TPU v7x, 128 devices: a whole 4x4x4 slice. The times are simulated.
128 devices in a mesh: att: 8 (over x, core), ffn: 16 (over y, z).
Axes of the slice: x: 4, y: 4, z: 4, core: 2. Of those that a mesh axis runs over, the one named last changes fastest.
Arguments:
- hidden: bfloat16 [4096, 7168], P(('att', 'ffn')), may hold values from -6 to 6
- route: int32 [4096, 1], P(('att', 'ffn')), may hold values from 0 to 7; in each aligned block of 32 rows (0 to 31, 32 to 63, ...) at most 8 rows name the same one
- norm_gain: float32 [7168], replicated, may hold values from 0.1 to 1.9
- gate_weight: bfloat16 [8, 7168, 9216], P('att', None, 'ffn'), may hold values from -0.0625 to 0.0625
- up_weight: bfloat16 [8, 7168, 9216], P('att', None, 'ffn'), may hold values from -0.0625 to 0.0625
- down_weight: bfloat16 [8, 9216, 7168], P('att', 'ffn'), may hold values from -0.0625 to 0.0625
Outputs:
- updated: bfloat16 [4096, 7168], P(('att', 'ffn'))
Inputs may be any that keep to these rules, and one draw needn't show every extreme that they name: `route`: among the 32 rows of one device no group is named by more than 8 rows.
All inputs are finite; a program needn't handle non-finite values.
Results may differ from a plain program's by a relative error of at most 0.014.
Values may be sent and summed in bfloat16 or wider, within the bound.
A program may use at most 128 MiB of HBM per device.

v0:
```python
import jax
import jax.numpy as jnp
from jax import lax
from jax.sharding import PartitionSpec as P


def per_device(hidden, route, norm_gain, gate_weight, up_weight, down_weight):
    groups = lax.axis_size("att")
    row_count = hidden.shape[0]
    capacity = 2 * row_count // groups
    widened = hidden.astype(jnp.float32)
    normed = (
        widened * lax.rsqrt(jnp.mean(widened * widened, axis=-1, keepdims=True) + 1e-06) * norm_gain
    ).astype(jnp.bfloat16)
    chosen = route[:, 0]
    member = (chosen[:, None] == jnp.arange(groups, dtype=jnp.int32)[None, :]).astype(jnp.int32)
    before = jnp.cumsum(member, axis=0) - member
    row_rank = jnp.sum(before * member, axis=1)
    row_slot = chosen * capacity + row_rank
    slot_table = (
        row_slot[:, None] == jnp.arange(groups * capacity, dtype=jnp.int32)[None, :]
    ).astype(jnp.bfloat16)
    outgoing = jnp.dot(slot_table.T, normed, preferred_element_type=jnp.float32).astype(
        jnp.bfloat16
    )
    w_gate = gate_weight[0]
    w_up = up_weight[0]
    w_down = down_weight[0]
    received = lax.all_to_all(outgoing, "att", split_axis=0, concat_axis=0, tiled=True)
    gathered = lax.all_gather(received, "ffn", axis=0, tiled=True)
    gate_act = jnp.dot(gathered, w_gate, preferred_element_type=jnp.float32)
    up_act = jnp.dot(gathered, w_up, preferred_element_type=jnp.float32)
    mid_act = (jax.nn.silu(gate_act) * up_act).astype(jnp.bfloat16)
    summed = lax.psum_scatter(
        jnp.dot(mid_act, w_down, preferred_element_type=jnp.float32).astype(jnp.bfloat16),
        "ffn",
        scatter_dimension=0,
        tiled=True,
    )
    returned = lax.all_to_all(summed, "att", split_axis=0, concat_axis=0, tiled=True)
    contribution = jnp.dot(slot_table, returned, preferred_element_type=jnp.float32)
    return (widened + contribution).astype(jnp.bfloat16)


def solution(mesh):
    placed = (
        P(("att", "ffn"), None),
        P(("att", "ffn"), None),
        P(),
        P("att", None, "ffn"),
        P("att", None, "ffn"),
        P("att", "ffn", None),
    )
    return jax.shard_map(
        per_device, mesh=mesh, in_specs=placed, out_specs=P(("att", "ffn"), None), check_vma=False
    )
```

profile of v0, /device:TPU:1, one launch (start us, length us, event | category | flops | bytes accessed | tf_op | source)
XLA Modules:
  0.0 303.6 jit_solution(17225461644826338731)
XLA Ops:
  6.5 0.0 all-gather.2.cloned.1.call-start
  6.5 1.2 fusion.9
  7.8 0.7 fusion.16
  8.5 0.1 reduce_window_sum.11
  8.6 0.8 select_reduce_fusion
  9.4 0.7 fusion.19
  10.1 1.5 fusion.5
  11.6 19.5 %all_to_all.24 = bf16[8,8,7168]{2,1,0:T(8,128)(2,1)} all-to-all(bf16[8,8,7168]{2,1,0:T(8,128)(2,1)S(1)} %fusion.5), channel_id=1, replica_groups=mesh['att'=8,'ffn'=16] {'att'}, dimensions={0} | all-to-all | bytes 1835008 | tf_op jit(solution)/shard_map/all_to_all | solution.py:29
  31.1 0.0 all-gather.2.cloned.1.call-update
  31.1 0.0 reduce-scatter.2.cloned.1.call-start
  31.2 101.6 %all-gather.2.cloned.1.call-done = bf16[1024,7168]{1,0:T(8,128)(2,1)} async-done(((bf16[64,7168]{1,0:T(8,128)(2,1)}), bf16[1024,7168]{1,0:T(8,128)(2,1)}) %all-gather.2.cloned.1.call-update) | async-done | bytes 14680080 | tf_op jit(solution)/shard_map/all_gather | solution.py:30
  132.7 0.0 copy-start.1
  132.7 13.3 %fusion.1 = f32[1024,576]{0,1:T(8,128)S(1)} fusion(bf16[1024,7168]{1,0:T(8,128)(2,1)} %all-gather.2.cloned.1.call-done, bf16[1,7168,576]{1,2,0:T(8,128)(2,1)} %param.10), kind=kOutput, calls=%fused_computation.2 | convolution fusion | flops 8455716864 | bytes 25296896 | tf_op jit(solution)/shard_map/dot_general | solution.py:32
  146.1 0.0 copy-done.1
  146.1 11.4 %multiply_convert_fusion = bf16[1024,576]{0,1:T(8,128)(2,1)S(1)} fusion(f32[1024,576]{0,1:T(8,128)S(1)} %fusion.1, bf16[1024,7168]{1,0:T(8,128)(2,1)S(1)} %copy-done.1, bf16[1,7168,576]{1,2,0:T(8,128)(2,1)} %param.9), kind=kOutput, calls=%fused_computation.10 | convolution fusion | flops 8459255808 | bytes 26476544 | tf_op jit(solution)/shard_map/dot_general | solution.py:31
  157.5 17.6 %convolution_convert_fusion = bf16[1024,7168]{1,0:T(8,128)(2,1)} fusion(bf16[1024,576]{0,1:T(8,128)(2,1)S(1)} %multiply_convert_fusion, bf16[1,576,7168]{2,1,0:T(8,128)(2,1)} %param.11), kind=kOutput, calls=%fused_computation | convolution fusion | flops 8463056896 | bytes 24117248 | tf_op jit(solution)/shard_map/dot_general | solution.py:35
  175.1 0.0 copy-start
  175.1 0.0 reduce-scatter.2.cloned.1.call-update
  175.2 101.4 %reduce-scatter.2.cloned.1.call-done = bf16[64,7168]{1,0:T(8,128)(2,1)} async-done(((bf16[1024,7168]{1,0:T(8,128)(2,1)}), bf16[64,7168]{1,0:T(8,128)(2,1)}) %reduce-scatter.2.cloned.1.call-update) | async-done | bytes 917520 | tf_op jit(solution)/shard_map/reduce_scatter | solution.py:34
  276.5 19.1 %all_to_all.25 = bf16[8,8,7168]{2,1,0:T(8,128)(2,1)S(1)} all-to-all(bf16[8,8,7168]{2,1,0:T(8,128)(2,1)} %bitcast.29), channel_id=1, replica_groups=mesh['att'=8,'ffn'=16] {'att'}, dimensions={0} | all-to-all | bytes 1835008 | tf_op jit(solution)/shard_map/all_to_all | solution.py:40
  295.6 0.0 copy-done
  295.6 1.1 fusion.6
  (1 shorter events, 0.0 us)
Async XLA Ops:
  6.5 126.2 %all-gather.2.cloned.1.call-start = ((), (), s32[]{:S(2)}) async-start(), calls=%async_computation.3 | async-start | bytes 15597568 | tf_op jit(solution)/shard_map/all_gather | solution.py:30
  31.1 245.4 %reduce-scatter.2.cloned.1.call-start = ((), (), s32[]{:S(2)}) async-start(), calls=%async_computation.4 | async-start | bytes 15597568 | tf_op jit(solution)/shard_map/reduce_scatter | solution.py:34
  132.7 13.3 %copy-start.1 = (bf16[1024,7168]{1,0:T(8,128)(2,1)S(1)}, bf16[1024,7168]{1,0:T(8,128)(2,1)}, u32[]{:S(2)}) copy-start(bf16[1024,7168]{1,0:T(8,128)(2,1)} %all-gather.2.cloned.1.call-done) | copy-start | bytes 44040196
  175.1 120.5 %copy-start = (bf16[32,7168]{1,0:T(8,128)(2,1)S(1)}, bf16[32,7168]{1,0:T(8,128)(2,1)}, u32[]{:S(2)}) copy-start(bf16[32,7168]{1,0:T(8,128)(2,1)} %param.6) | copy-start | bytes 1376260
Sparse Core Ops, SparseCore 0:
  31.2 101.4 all-gather.1
  175.3 101.2 reduce-scatter.1
where the time goes:
time: 304 us
  waiting for transfers between devices  203 us (67%)
  matrix products  45 us (15%)
  blocking collectives  38.6 us (13%)
  between operations  13.4 us (4%)
  other arithmetic  3.51 us (1%)
    all_gather x1, waiting for transfers between devices, per_device(): gathered = lax.all_gather(received, 'ffn', axis=0, tiled=True)  102 us
    reduce_scatter x1, waiting for transfers between devices, per_device(): lax.psum_scatter(jnp.dot(mid_act, w_down, preferred_element_type=jnp.floa...  101 us
    all_to_all x1, blocking collectives, per_device(): lax.all_to_all(outgoing, 'att', split_axis=0, concat_axis=0, tiled=True)  19.5 us
    all_to_all x1, blocking collectives, per_device(): lax.all_to_all(summed, 'att', split_axis=0, concat_axis=0, tiled=True)  19.1 us
    dot_general x1, matrix products, per_device(): jnp.dot(mid_act, w_down, preferred_element_type=jnp.float32)  17.6 us
    dot_general x1, matrix products, per_device(): up_act = jnp.dot(gathered, w_up, preferred_element_type=jnp.float32)  13.3 us
    dot_general x1, matrix products, per_device(): gate_act = jnp.dot(gathered, w_gate, preferred_element_type=jnp.float32)  11.4 us
  transfers between devices with their start and end apart: 2, of which 2 were waited for; matrix products, arithmetic and copies ran while one was open for 0% of the time, Pallas kernels for 0%

commit v1 on v0

v1 whole, which is shorter than its diff:
```python
import jax
import jax.numpy as jnp
from jax import lax
from jax.experimental import pallas as pl
from jax.experimental.pallas import tpu as pltpu
from jax.sharding import PartitionSpec as P

MESH = pl.DeviceIdType.MESH
F32 = jnp.float32
BF16 = jnp.bfloat16


def chip_offset(part):
    return part + part // 2 - 2 * (part // 3)


def ffn_kernel(
    hidden, route, gain, gate_hbm, up_hbm, down_hbm, out,
    w_gate, w_up, w_down, blocks_out, blocks_in, blocks_back, returned, rows, gate_sum, up_sum, mid,
    near_y1, near_z1, near_y2, near_z2, far_z1, far_y1, far_z2, far_y2,
    w_sem, in_send, in_recv, back_send, back_recv, gather_send, gather_recv, reduce_send, reduce_recv,
):
    att, ffn = lax.axis_index("att"), lax.axis_index("ffn")
    x, core = att // 2, att % 2
    y, z = ffn // 4, ffn % 4
    yp, y2, ym = (y + 1) % 4, (y + 2) % 4, (y + 3) % 4
    zp, z2, zm = (z + 1) % 4, (z + 2) % 4, (z + 3) % 4
    width = hidden.shape[1]
    half, quarter = width // 2, width // 4
    a_cols, b_cols = pl.ds(0, half), pl.ds(half, half)
    q = [pl.ds(i * quarter, quarter) for i in range(4)]
    z_plus, z_minus, y_plus, y_minus = (att, y * 4 + zp), (att, y * 4 + zm), (att, yp * 4 + z), (att, ym * 4 + z)
    ALL = pl.ds(0, 4)

    barrier = pltpu.get_barrier_semaphore()
    for other in (z_plus, z_minus, y_plus, y_minus):
        pl.semaphore_signal(barrier, inc=1, device_id=other, device_id_type=MESH)
    for step in range(1, 8):
        pl.semaphore_signal(barrier, inc=1, device_id=((att + step) % 8, ffn), device_id_type=MESH)
    loads = [
        pltpu.make_async_copy(src.at[0], dst, w_sem.at[i])
        for i, (src, dst) in enumerate(((gate_hbm, w_gate), (up_hbm, w_up), (down_hbm, w_down)))
    ]
    for load in loads:
        load.start()

    widened = hidden[...].astype(F32)
    scale = lax.rsqrt(jnp.mean(widened * widened, axis=-1, keepdims=True) + 1e-06)
    normed = (widened * scale * gain[...]).astype(BF16)
    lane = lax.broadcasted_iota(jnp.int32, (32, 128), 1)
    member = (lane == route[...]).astype(F32)
    earlier = (
        lax.broadcasted_iota(jnp.int32, (32, 32), 1) < lax.broadcasted_iota(jnp.int32, (32, 32), 0)
    ).astype(F32)
    before = jnp.dot(earlier, member, preferred_element_type=F32)
    rank = jnp.sum(before * member, axis=1, keepdims=True).astype(jnp.int32)
    place = route[...] * 16 + rank
    table_a = (lane == place).astype(F32).astype(BF16)
    table_b = (lane == place + 8).astype(F32).astype(BF16)
    turned = (((0,), (0,)), ((), ()))
    placed = lax.dot_general(table_a, normed[:, :half], turned, preferred_element_type=F32)
    placed = placed + lax.dot_general(table_b, normed[:, half:], turned, preferred_element_type=F32)
    blocks_out[...] = placed.astype(BF16).reshape(8, 16, half)

    pl.semaphore_wait(barrier, 11)

    def in_copy(part, to_core):
        dest = ((x + 4 - chip_offset(part)) % 4) * 2 + to_core
        return pltpu.make_async_remote_copy(
            src_ref=blocks_out.at[dest], dst_ref=blocks_in.at[part, core],
            send_sem=in_send.at[part, to_core], recv_sem=in_recv.at[part, core],
            device_id=(dest, ffn), device_id_type=MESH,
        )

    in_copy(0, 1 - core).start()
    for part in range(1, 4):
        for to_core in range(2):
            in_copy(part, to_core).start()
    blocks_in[0, core] = blocks_out[att]

    def wait_in(part, from_core):
        pltpu.make_async_copy(blocks_out.at[0], blocks_in.at[part, from_core], in_recv.at[part, from_core]).wait()

    LINK = {0: z_plus, 1: z_minus, 2: y_plus, 3: y_minus}

    def g_send(part, link, event, at_y, at_z, cols):
        piece = rows.at[part, at_y, at_z, :, cols]
        pltpu.make_async_remote_copy(
            src_ref=piece, dst_ref=piece,
            send_sem=gather_send.at[part, event], recv_sem=gather_recv.at[part, link, event],
            device_id=LINK[link], device_id_type=MESH,
        ).start()

    def g_wait(part, link, event, cols):
        piece = rows.at[part, 0, 0, :, cols]
        pltpu.make_async_copy(piece, piece, gather_recv.at[part, link, event]).wait()

    whole = pl.ds(0, width)

    def gather_own(part):
        @pl.when(part == 0)
        def _():
            wait_in(0, 1 - core)

        @pl.when(part > 0)
        def _():
            wait_in(part, 0)
            wait_in(part, 1)

        first, second = blocks_in[part, 0].astype(F32), blocks_in[part, 1].astype(F32)
        rows[part, y, z, :, a_cols] = jnp.concatenate([first[:8], second[:8]], axis=0).astype(BF16)
        rows[part, y, z, :, b_cols] = jnp.concatenate([first[8:], second[8:]], axis=0).astype(BF16)
        for link in range(4):
            g_send(part, link, 0, y, z, whole)

    def gather_a(part):
        for link in range(4):
            g_wait(part, link, 0, whole)
        g_send(part, 0, 1, y, zm, q[0])
        g_send(part, 1, 1, y, zp, q[1])
        g_send(part, 2, 1, ym, z, q[2])
        g_send(part, 3, 1, yp, z, q[3])
        for link in (2, 3):
            g_send(part, link, 2, y, zm, a_cols)
        for link in (0, 1):
            g_send(part, link, 2, ym, z, b_cols)
        for link in (2, 3):
            g_send(part, link, 3, y, zp, a_cols)
        for link in (0, 1):
            g_send(part, link, 3, yp, z, b_cols)
        g_send(part, 0, 5, y, zm, q[2])
        g_send(part, 1, 5, y, zp, q[3])
        g_send(part, 2, 5, ym, z, q[0])
        g_send(part, 3, 5, yp, z, q[1])

    def gather_b(part):
        for link in range(4):
            g_wait(part, link, 1, q[0])
        for link in (2, 3):
            g_send(part, link, 4, y, z2, a_cols)
        for link in (0, 1):
            g_send(part, link, 4, y2, z, b_cols)

    def gather_on(part, event, of_y, of_z):
        for link in range(4):
            g_wait(part, link, event, a_cols)
        g_send(part, 0, event + 4, of_y, zm, q[2])
        g_send(part, 1, event + 4, of_y, zp, q[3])
        g_send(part, 2, event + 4, ym, of_z, q[0])
        g_send(part, 3, event + 4, yp, of_z, q[1])

    def gather_c(part):
        gather_on(part, 2, ym, zm)
        gather_on(part, 3, yp, zp)

    def gather_d(part):
        gather_on(part, 4, y2, z2)

    def gather_e(part):
        for event in range(5, 9):
            for link in range(4):
                g_wait(part, link, event, q[0])

    def wait_units(sem, part, units):
        piece = rows.at[part, 0, pl.ds(0, units)] if units <= 4 else rows.at[part, pl.ds(0, units // 4)]
        pltpu.make_async_copy(piece, piece, sem).wait()

    def gather_sent(part):
        for event, units in enumerate((4, 1, 2, 2, 2, 1, 1, 1, 1)):
            wait_units(gather_send.at[part, event], part, units)

    def project(part, lower, upper):
        @pl.loop(lower, upper)
        def _(i):
            cols = pl.ds(pl.multiple_of(i * quarter, quarter), quarter)
            block = rows[part, :, :, :, cols].reshape(256, quarter)
            gate = jnp.dot(block, w_gate[cols, :], preferred_element_type=F32)
            up = jnp.dot(block, w_up[cols, :], preferred_element_type=F32)

            @pl.when(i == 0)
            def _():
                gate_sum[...] = gate
                up_sum[...] = up

            @pl.when(i > 0)
            def _():
                gate_sum[...] += gate
                up_sum[...] += up

    def activate():
        gate = gate_sum[...]
        mid[...] = (gate / (1.0 + jnp.exp(-gate)) * up_sum[...]).astype(BF16)

    def lower_rows(part, lower, upper):
        @pl.loop(lower, upper)
        def _(i):
            cols = pl.ds(pl.multiple_of(i * quarter, quarter), quarter)
            partial = jnp.dot(mid[...], w_down[:, cols], preferred_element_type=F32)
            rows[part, :, :, :, cols] = partial.astype(BF16).reshape(4, 4, 16, quarter)

    def r_send(part, link, event, src, dst):
        pltpu.make_async_remote_copy(
            src_ref=src, dst_ref=dst,
            send_sem=reduce_send.at[part, event], recv_sem=reduce_recv.at[part, link, event],
            device_id=LINK[link], device_id_type=MESH,
        ).start()

    def r_wait(part, link, event, dst):
        pltpu.make_async_copy(dst, dst, reduce_recv.at[part, link, event]).wait()

    def add(index, *terms):
        total = rows[index].astype(F32)
        for term in terms:
            total = total + term.astype(F32)
        rows[index] = total.astype(BF16)

    def reduce_1(part):
        r_send(part, 2, 0, rows.at[part, y2, :, :, q[0]], near_y1.at[part, 0])
        r_send(part, 3, 0, rows.at[part, y2, :, :, q[1]], near_y1.at[part, 1])
        r_send(part, 0, 0, rows.at[part, :, z2, :, q[2]], near_z1.at[part, 0])
        r_send(part, 1, 0, rows.at[part, :, z2, :, q[3]], near_z1.at[part, 1])

    def reduce_2(part):
        r_wait(part, 2, 0, near_y1.at[part, 0])
        add((part, yp, ALL, slice(None), q[0]), near_y1[part, 0])
        r_send(part, 2, 1, rows.at[part, yp, :, :, a_cols], near_y2.at[part, 0])
        r_wait(part, 3, 0, near_y1.at[part, 1])
        add((part, ym, ALL, slice(None), q[1]), near_y1[part, 1])
        r_send(part, 3, 1, rows.at[part, ym, :, :, a_cols], near_y2.at[part, 1])
        r_wait(part, 0, 0, near_z1.at[part, 0])
        add((part, ALL, zp, slice(None), q[2]), near_z1[part, 0])
        r_send(part, 0, 1, rows.at[part, :, zp, :, b_cols], near_z2.at[part, 0])
        r_wait(part, 1, 0, near_z1.at[part, 1])
        add((part, ALL, zm, slice(None), q[3]), near_z1[part, 1])
        r_send(part, 1, 1, rows.at[part, :, zm, :, b_cols], near_z2.at[part, 1])

    def reduce_3(part):
        r_wait(part, 2, 1, near_y2.at[part, 0])
        r_wait(part, 3, 1, near_y2.at[part, 1])
        add((part, y, ALL, slice(None), a_cols), near_y2[part, 0], near_y2[part, 1])
        r_send(part, 0, 2, rows.at[part, y, z2, :, q[0]], far_z1.at[part, 0])
        r_send(part, 1, 2, rows.at[part, y, z2, :, q[1]], far_z1.at[part, 1])
        r_wait(part, 0, 1, near_z2.at[part, 0])
        r_wait(part, 1, 1, near_z2.at[part, 1])
        add((part, ALL, z, slice(None), b_cols), near_z2[part, 0], near_z2[part, 1])
        r_send(part, 2, 2, rows.at[part, y2, z, :, q[2]], far_y1.at[part, 0])
        r_send(part, 3, 2, rows.at[part, y2, z, :, q[3]], far_y1.at[part, 1])

    def reduce_4(part):
        r_wait(part, 0, 2, far_z1.at[part, 0])
        add((part, y, zp, slice(None), q[0]), far_z1[part, 0])
        r_send(part, 0, 3, rows.at[part, y, zp, :, a_cols], far_z2.at[part, 0])
        r_wait(part, 1, 2, far_z1.at[part, 1])
        add((part, y, zm, slice(None), q[1]), far_z1[part, 1])
        r_send(part, 1, 3, rows.at[part, y, zm, :, a_cols], far_z2.at[part, 1])
        r_wait(part, 2, 2, far_y1.at[part, 0])
        add((part, yp, z, slice(None), q[2]), far_y1[part, 0])
        r_send(part, 2, 3, rows.at[part, yp, z, :, b_cols], far_y2.at[part, 0])
        r_wait(part, 3, 2, far_y1.at[part, 1])
        add((part, ym, z, slice(None), q[3]), far_y1[part, 1])
        r_send(part, 3, 3, rows.at[part, ym, z, :, b_cols], far_y2.at[part, 1])

    def back_copy(part, to_core):
        dest = ((x + chip_offset(part)) % 4) * 2 + to_core
        return pltpu.make_async_remote_copy(
            src_ref=blocks_back.at[part, to_core], dst_ref=returned.at[att],
            send_sem=back_send.at[part, to_core], recv_sem=back_recv.at[att],
            device_id=(dest, ffn), device_id_type=MESH,
        )

    def reduce_5(part):
        for side in range(2):
            r_wait(part, side, 3, far_z2.at[part, side])
            r_wait(part, 2 + side, 3, far_y2.at[part, side])
        left = rows[part, y, z, :, a_cols].astype(F32) + far_z2[part, 0].astype(F32) + far_z2[part, 1].astype(F32)
        right = rows[part, y, z, :, b_cols].astype(F32) + far_y2[part, 0].astype(F32) + far_y2[part, 1].astype(F32)
        for to_core in range(2):
            lines = slice(8 * to_core, 8 * to_core + 8)
            blocks_back[part, to_core] = jnp.concatenate([left[lines], right[lines]], axis=0).astype(BF16)

        @pl.when(part == 0)
        def _():
            back_copy(part, 1 - core).start()
            returned[att] = blocks_back[0, core]

        @pl.when(part > 0)
        def _():
            back_copy(part, 0).start()
            back_copy(part, 1).start()

        for event, units in enumerate((4, 8, 1, 2)):
            wait_units(reduce_send.at[part, event], part, units)

    gather_own(0)
    for load in loads:
        load.wait()

    @pl.loop(0, 6)
    def _(step):
        gathering = step < 4
        computing = jnp.logical_and(step >= 1, step < 5)
        reducing = step >= 2
        at_c, at_r = step - 1, step - 2

        @pl.when(reducing)
        def _():
            reduce_2(at_r)

        @pl.when(gathering)
        def _():
            gather_a(step)

        @pl.when(computing)
        def _():
            project(at_c, 0, 2)

        @pl.when(gathering)
        def _():
            gather_b(step)

        @pl.when(computing)
        def _():
            project(at_c, 2, 4)

        @pl.when(gathering)
        def _():
            gather_c(step)

        @pl.when(step < 3)
        def _():
            gather_own(step + 1)

        @pl.when(reducing)
        def _():
            reduce_3(at_r)

        @pl.when(computing)
        def _():
            activate()
            gather_sent(at_c)
            lower_rows(at_c, 0, 2)

        @pl.when(gathering)
        def _():
            gather_d(step)

        @pl.when(reducing)
        def _():
            reduce_4(at_r)

        @pl.when(computing)
        def _():
            lower_rows(at_c, 2, 4)

        @pl.when(gathering)
        def _():
            gather_e(step)

        @pl.when(computing)
        def _():
            reduce_1(at_c)

        @pl.when(reducing)
        def _():
            reduce_5(at_r)

    in_copy(0, 1 - core).wait_send()
    back_copy(0, 1 - core).wait_send()
    for part in range(1, 4):
        for to_core in range(2):
            in_copy(part, to_core).wait_send()
            back_copy(part, to_core).wait_send()
    for step in range(1, 8):
        source = (att + step) % 8
        pltpu.make_async_copy(blocks_out.at[0], returned.at[source], back_recv.at[source]).wait()
    lines = returned[...].reshape(128, half)
    out[:, :half] = (
        hidden[:, :half].astype(F32) + jnp.dot(table_a, lines, preferred_element_type=F32)
    ).astype(BF16)
    out[:, half:] = (
        hidden[:, half:].astype(F32) + jnp.dot(table_b, lines, preferred_element_type=F32)
    ).astype(BF16)


def per_device(hidden, route, norm_gain, gate_weight, up_weight, down_weight):
    row_count, width = hidden.shape
    units = gate_weight.shape[2]
    half, quarter = width // 2, width // 4
    vmem, dma = pltpu.VMEM, pltpu.SemaphoreType.DMA
    return pl.pallas_call(
        ffn_kernel,
        out_shape=jax.ShapeDtypeStruct((row_count, width), BF16),
        in_specs=[pl.BlockSpec(memory_space=vmem)] * 3 + [pl.BlockSpec(memory_space=pl.ANY)] * 3,
        out_specs=pl.BlockSpec(memory_space=vmem),
        scratch_shapes=[
            vmem((width, units), BF16),
            vmem((width, units), BF16),
            vmem((units, width), BF16),
            vmem((8, 16, half), BF16),
            vmem((4, 2, 16, half), BF16),
            vmem((4, 2, 16, half), BF16),
            vmem((8, 16, half), BF16),
            vmem((4, 4, 4, 16, width), BF16),
            vmem((256, units), F32),
            vmem((256, units), F32),
            vmem((256, units), BF16),
            vmem((4, 2, 4, 16, quarter), BF16),
            vmem((4, 2, 4, 16, quarter), BF16),
            vmem((4, 2, 4, 16, half), BF16),
            vmem((4, 2, 4, 16, half), BF16),
            vmem((4, 2, 16, quarter), BF16),
            vmem((4, 2, 16, quarter), BF16),
            vmem((4, 2, 16, half), BF16),
            vmem((4, 2, 16, half), BF16),
            dma((3,)),
            dma((4, 2)),
            dma((4, 2)),
            dma((4, 2)),
            dma((8,)),
            dma((4, 9)),
            dma((4, 4, 9)),
            dma((4, 4)),
            dma((4, 4, 4)),
        ],
        compiler_params=pltpu.CompilerParams(
            collective_id=0, has_side_effects=True, vmem_limit_bytes=62 * 1024 * 1024
        ),
    )(hidden, route, norm_gain.reshape(1, width), gate_weight, up_weight, down_weight)


def solution(mesh):
    placed = (
        P(("att", "ffn"), None),
        P(("att", "ffn"), None),
        P(),
        P("att", None, "ffn"),
        P("att", None, "ffn"),
        P("att", "ffn", None),
    )
    return jax.shard_map(
        per_device, mesh=mesh, in_specs=placed, out_specs=P(("att", "ffn"), None), check_vma=False
    )
```

time: 304 us -> 220 us (0.72)
  waiting for transfers between devices: 203 us -> 0 us
  Pallas kernels: 0 us -> 192 us
  matrix products: 45 us -> 0 us
  blocking collectives: 38.6 us -> 0 us
  local copies, waits for them, and re-layouts: 0.01 us -> 27.9 us
  between operations: 13.4 us -> 0.01 us
  other arithmetic: 3.51 us -> 0 us
    pallas_call x0 -> x1, Pallas kernels: none -> 192 us  [per_device(): pl.pallas_call(ffn_kernel, out_shape=jax.ShapeDtypeStruct((row_count, wid...]
    all_gather x1 -> x0, waiting for transfers between devices: 102 us -> none  [per_device(): gathered = lax.all_gather(received, 'ffn', axis=0, tiled=True)]
    reduce_scatter x1 -> x0, waiting for transfers between devices: 101 us -> none  [per_device(): lax.psum_scatter(jnp.dot(mid_act, w_down, preferred_element_type=jnp.floa...]
    dot_general x5 -> x0, matrix products: 45 us -> none  [the longest x1 17.6 us: per_device(): jnp.dot(mid_act, w_down, preferred_element_type=jnp.float32)]
    all_to_all x2 -> x0, blocking collectives: 38.6 us -> none  [the longest x1 19.5 us: per_device(): lax.all_to_all(outgoing, 'att', split_axis=0, concat_axis=0, tiled=True)]
    unnamed x4, local copies, waits for them, and re-layouts: 0.01 us -> 27.9 us
  transfers between devices with their start and end apart: 2 -> 0, of which waited for: 2 -> 0; matrix products, arithmetic and copies ran while one was open for 0% -> 0% of each run, Pallas kernels for 0% -> 0%
where the time goes in v1:
time: 220 us
  Pallas kernels  192 us (87%)
  local copies, waits for them, and re-layouts  27.9 us (13%)
    pallas_call x1, Pallas kernels, per_device(): pl.pallas_call(ffn_kernel, out_shape=jax.ShapeDtypeStruct((row_count, wid...  192 us
    unnamed x4, local copies, waits for them, and re-layouts  27.9 us

profile of v1, /device:TPU:1, one launch (start us, length us, event | category | flops | bytes accessed | tf_op | source)
XLA Modules:
  0.0 219.7 jit_solution(12155223186450846121)
XLA Ops:
  0.0 1.3 copy.7.route
  1.3 12.4 %copy.8.gate_hbm = bf16[1,7168,576]{2,1,0:T(8,128)(2,1)} copy(bf16[1,7168,576]{1,2,0:T(8,128)(2,1)} %param.9) | data formatting | bytes 16515072 | tf_op args[3]
  13.7 12.4 %copy.9.up_hbm = bf16[1,7168,576]{2,1,0:T(8,128)(2,1)} copy(bf16[1,7168,576]{1,2,0:T(8,128)(2,1)} %param.10) | data formatting | bytes 16515072 | tf_op args[4]
  26.1 191.8 %shard_map.64 = bf16[32,7168]{1,0:T(8,128)(2,1)} custom-call(bf16[32,7168]{1,0:T(8,128)(2,1)} %hidden.1, s32[32,1]{1,0:T(8,128)} %copy.7.route, f32[1,7168]{1,0:T(1,128)} %bitcast.1, bf16[1,7168,576]{2,1,0:T(8,128)(2,1)} %copy.8.gate_hbm, bf16[1,7168,576]{2,1,0:T(8,128)(2,1)} %copy.9.up_hbm, bf16[1,576,7168]{2,1,0:T(8,128)(2,1)} %down_hbm.1), custom_call_target="tpu_custom_call" | custom-call | tf_op jit(solution)/shard_map/pallas_call | solution.py:390
  217.9 1.8 copy.11

commit v2 on v1

--- a/solution.py
+++ b/solution.py
@@ -8,6 +8,8 @@
 MESH = pl.DeviceIdType.MESH
 F32 = jnp.float32
 BF16 = jnp.bfloat16
+FIRST = (((0,), (0,)), ((), ()))
+LAST = (((1,), (1,)), ((), ()))
 
 
 def chip_offset(part):
@@ -47,19 +49,18 @@
     widened = hidden[...].astype(F32)
     scale = lax.rsqrt(jnp.mean(widened * widened, axis=-1, keepdims=True) + 1e-06)
     normed = (widened * scale * gain[...]).astype(BF16)
-    lane = lax.broadcasted_iota(jnp.int32, (32, 128), 1)
-    member = (lane == route[...]).astype(F32)
+    member = (lax.broadcasted_iota(jnp.int32, (8, 32), 0) == route[...]).astype(F32)
     earlier = (
-        lax.broadcasted_iota(jnp.int32, (32, 32), 1) < lax.broadcasted_iota(jnp.int32, (32, 32), 0)
+        lax.broadcasted_iota(jnp.int32, (32, 32), 0) < lax.broadcasted_iota(jnp.int32, (32, 32), 1)
     ).astype(F32)
-    before = jnp.dot(earlier, member, preferred_element_type=F32)
-    rank = jnp.sum(before * member, axis=1, keepdims=True).astype(jnp.int32)
+    before = jnp.dot(member, earlier, preferred_element_type=F32)
+    rank = jnp.sum(before * member, axis=0, keepdims=True).astype(jnp.int32)
     place = route[...] * 16 + rank
-    table_a = (lane == place).astype(F32).astype(BF16)
-    table_b = (lane == place + 8).astype(F32).astype(BF16)
-    turned = (((0,), (0,)), ((), ()))
-    placed = lax.dot_general(table_a, normed[:, :half], turned, preferred_element_type=F32)
-    placed = placed + lax.dot_general(table_b, normed[:, half:], turned, preferred_element_type=F32)
+    line = lax.broadcasted_iota(jnp.int32, (128, 32), 0)
+    table_a = (line == place).astype(F32).astype(BF16)
+    table_b = (line == place + 8).astype(F32).astype(BF16)
+    placed = jnp.dot(table_a, normed[:, :half], preferred_element_type=F32)
+    placed = placed + jnp.dot(table_b, normed[:, half:], preferred_element_type=F32)
     blocks_out[...] = placed.astype(BF16).reshape(8, 16, half)
 
     pl.semaphore_wait(barrier, 11)
@@ -174,8 +175,8 @@
         def _(i):
             cols = pl.ds(pl.multiple_of(i * quarter, quarter), quarter)
             block = rows[part, :, :, :, cols].reshape(256, quarter)
-            gate = jnp.dot(block, w_gate[cols, :], preferred_element_type=F32)
-            up = jnp.dot(block, w_up[cols, :], preferred_element_type=F32)
+            gate = lax.dot_general(block, w_gate[:, cols], LAST, preferred_element_type=F32)
+            up = lax.dot_general(block, w_up[:, cols], LAST, preferred_element_type=F32)
 
             @pl.when(i == 0)
             def _():
@@ -292,8 +293,6 @@
             wait_units(reduce_send.at[part, event], part, units)
 
     gather_own(0)
-    for load in loads:
-        load.wait()
 
     @pl.loop(0, 6)
     def _(step):
@@ -309,6 +308,11 @@
         @pl.when(gathering)
         def _():
             gather_a(step)
+
+        @pl.when(step == 1)
+        def _():
+            for load in loads:
+                load.wait()
 
         @pl.when(computing)
         def _():
@@ -375,10 +379,10 @@
         pltpu.make_async_copy(blocks_out.at[0], returned.at[source], back_recv.at[source]).wait()
     lines = returned[...].reshape(128, half)
     out[:, :half] = (
-        hidden[:, :half].astype(F32) + jnp.dot(table_a, lines, preferred_element_type=F32)
+        hidden[:, :half].astype(F32) + lax.dot_general(table_a, lines, FIRST, preferred_element_type=F32)
     ).astype(BF16)
     out[:, half:] = (
-        hidden[:, half:].astype(F32) + jnp.dot(table_b, lines, preferred_element_type=F32)
+        hidden[:, half:].astype(F32) + lax.dot_general(table_b, lines, FIRST, preferred_element_type=F32)
     ).astype(BF16)
 
 
@@ -393,8 +397,8 @@
         in_specs=[pl.BlockSpec(memory_space=vmem)] * 3 + [pl.BlockSpec(memory_space=pl.ANY)] * 3,
         out_specs=pl.BlockSpec(memory_space=vmem),
         scratch_shapes=[
-            vmem((width, units), BF16),
-            vmem((width, units), BF16),
+            vmem((units, width), BF16),
+            vmem((units, width), BF16),
             vmem((units, width), BF16),
             vmem((8, 16, half), BF16),
             vmem((4, 2, 16, half), BF16),
@@ -425,7 +429,10 @@
         compiler_params=pltpu.CompilerParams(
             collective_id=0, has_side_effects=True, vmem_limit_bytes=62 * 1024 * 1024
         ),
-    )(hidden, route, norm_gain.reshape(1, width), gate_weight, up_weight, down_weight)
+    )(
+        hidden, route.reshape(1, row_count), norm_gain.reshape(1, width),
+        jnp.swapaxes(gate_weight, 1, 2), jnp.swapaxes(up_weight, 1, 2), down_weight,
+    )
 
 
 def solution(mesh):

time: 220 us -> 194 us (0.88)
  local copies, waits for them, and re-layouts: 27.9 us -> 1.82 us
    unnamed x4 -> x1, local copies, waits for them, and re-layouts: 27.9 us -> 1.82 us
where the time goes in v2:
time: 194 us
  Pallas kernels  192 us (99%)
    pallas_call x1, Pallas kernels, per_device(): pl.pallas_call(ffn_kernel, out_shape=jax.ShapeDtypeStruct((row_count, wid...  192 us

profile of v2, /device:TPU:1, one launch (start us, length us, event | category | flops | bytes accessed | tf_op | source)
XLA Modules:
  0.0 193.6 jit_solution(17639854364452325586)
XLA Ops:
  0.0 191.8 %shard_map.64 = bf16[32,7168]{1,0:T(8,128)(2,1)} custom-call(bf16[32,7168]{1,0:T(8,128)(2,1)} %hidden.1, s32[1,32]{1,0:T(1,128)} %bitcast.7, f32[1,7168]{1,0:T(1,128)} %bitcast.6, bf16[1,576,7168]{2,1,0:T(8,128)(2,1)} %bitcast.4, bf16[1,576,7168]{2,1,0:T(8,128)(2,1)} %bitcast.5, bf16[1,576,7168]{2,1,0:T(8,128)(2,1)} %down_hbm.1), custom_call_target="tpu_custom_call" | custom-call | tf_op jit(solution)/shard_map/pallas_call | solution.py:394
  191.8 1.8 copy.8

commit v3 on v2

--- a/solution.py
+++ b/solution.py
@@ -10,10 +10,6 @@
 BF16 = jnp.bfloat16
 FIRST = (((0,), (0,)), ((), ()))
 LAST = (((1,), (1,)), ((), ()))
-
-
-def chip_offset(part):
-    return part + part // 2 - 2 * (part // 3)
 
 
 def ffn_kernel(
@@ -66,7 +62,7 @@
     pl.semaphore_wait(barrier, 11)
 
     def in_copy(part, to_core):
-        dest = ((x + 4 - chip_offset(part)) % 4) * 2 + to_core
+        dest = ((x + 4 - part) % 4) * 2 + to_core
         return pltpu.make_async_remote_copy(
             src_ref=blocks_out.at[dest], dst_ref=blocks_in.at[part, core],
             send_sem=in_send.at[part, to_core], recv_sem=in_recv.at[part, core],
@@ -175,8 +171,8 @@
         def _(i):
             cols = pl.ds(pl.multiple_of(i * quarter, quarter), quarter)
             block = rows[part, :, :, :, cols].reshape(256, quarter)
-            gate = lax.dot_general(block, w_gate[:, cols], LAST, preferred_element_type=F32)
-            up = lax.dot_general(block, w_up[:, cols], LAST, preferred_element_type=F32)
+            gate = lax.dot_general(w_gate[:, cols], block, LAST, preferred_element_type=F32)
+            up = lax.dot_general(w_up[:, cols], block, LAST, preferred_element_type=F32)
 
             @pl.when(i == 0)
             def _():
@@ -190,7 +186,7 @@
 
     def activate():
         gate = gate_sum[...]
-        mid[...] = (gate / (1.0 + jnp.exp(-gate)) * up_sum[...]).astype(BF16)
+        mid[...] = (gate / (1.0 + jnp.exp(-gate)) * up_sum[...]).T.astype(BF16)
 
     def lower_rows(part, lower, upper):
         @pl.loop(lower, upper)
@@ -202,7 +198,7 @@
     def r_send(part, link, event, src, dst):
         pltpu.make_async_remote_copy(
             src_ref=src, dst_ref=dst,
-            send_sem=reduce_send.at[part, event], recv_sem=reduce_recv.at[part, link, event],
+            send_sem=reduce_send.at[part, 3 if event == 9 else event // 4], recv_sem=reduce_recv.at[part, link, event],
             device_id=LINK[link], device_id_type=MESH,
         ).start()
 
@@ -215,54 +211,54 @@
             total = total + term.astype(F32)
         rows[index] = total.astype(BF16)
 
-    def reduce_1(part):
-        r_send(part, 2, 0, rows.at[part, y2, :, :, q[0]], near_y1.at[part, 0])
-        r_send(part, 3, 0, rows.at[part, y2, :, :, q[1]], near_y1.at[part, 1])
-        r_send(part, 0, 0, rows.at[part, :, z2, :, q[2]], near_z1.at[part, 0])
-        r_send(part, 1, 0, rows.at[part, :, z2, :, q[3]], near_z1.at[part, 1])
+    across_z, across_y = (z2, zp, zm, z), (y2, yp, ym, y)
+
+    def reduce_1a(part):
+        for i in range(4):
+            r_send(part, 2, i, rows.at[part, y2, across_z[i], :, q[0]], near_y1.at[part, 0, i])
+            r_send(part, 3, i, rows.at[part, y2, across_z[i], :, q[1]], near_y1.at[part, 1, i])
+
+    def reduce_1b(part):
+        for i in range(4):
+            r_send(part, 0, i, rows.at[part, across_y[i], z2, :, q[2]], near_z1.at[part, 0, i])
+            r_send(part, 1, i, rows.at[part, across_y[i], z2, :, q[3]], near_z1.at[part, 1, i])
 
     def reduce_2(part):
-        r_wait(part, 2, 0, near_y1.at[part, 0])
-        add((part, yp, ALL, slice(None), q[0]), near_y1[part, 0])
-        r_send(part, 2, 1, rows.at[part, yp, :, :, a_cols], near_y2.at[part, 0])
-        r_wait(part, 3, 0, near_y1.at[part, 1])
-        add((part, ym, ALL, slice(None), q[1]), near_y1[part, 1])
-        r_send(part, 3, 1, rows.at[part, ym, :, :, a_cols], near_y2.at[part, 1])
-        r_wait(part, 0, 0, near_z1.at[part, 0])
-        add((part, ALL, zp, slice(None), q[2]), near_z1[part, 0])
-        r_send(part, 0, 1, rows.at[part, :, zp, :, b_cols], near_z2.at[part, 0])
-        r_wait(part, 1, 0, near_z1.at[part, 1])
-        add((part, ALL, zm, slice(None), q[3]), near_z1[part, 1])
-        r_send(part, 1, 1, rows.at[part, :, zm, :, b_cols], near_z2.at[part, 1])
-
-    def reduce_3(part):
-        r_wait(part, 2, 1, near_y2.at[part, 0])
-        r_wait(part, 3, 1, near_y2.at[part, 1])
-        add((part, y, ALL, slice(None), a_cols), near_y2[part, 0], near_y2[part, 1])
-        r_send(part, 0, 2, rows.at[part, y, z2, :, q[0]], far_z1.at[part, 0])
-        r_send(part, 1, 2, rows.at[part, y, z2, :, q[1]], far_z1.at[part, 1])
-        r_wait(part, 0, 1, near_z2.at[part, 0])
-        r_wait(part, 1, 1, near_z2.at[part, 1])
-        add((part, ALL, z, slice(None), b_cols), near_z2[part, 0], near_z2[part, 1])
-        r_send(part, 2, 2, rows.at[part, y2, z, :, q[2]], far_y1.at[part, 0])
-        r_send(part, 3, 2, rows.at[part, y2, z, :, q[3]], far_y1.at[part, 1])
-
-    def reduce_4(part):
-        r_wait(part, 0, 2, far_z1.at[part, 0])
-        add((part, y, zp, slice(None), q[0]), far_z1[part, 0])
-        r_send(part, 0, 3, rows.at[part, y, zp, :, a_cols], far_z2.at[part, 0])
-        r_wait(part, 1, 2, far_z1.at[part, 1])
-        add((part, y, zm, slice(None), q[1]), far_z1[part, 1])
-        r_send(part, 1, 3, rows.at[part, y, zm, :, a_cols], far_z2.at[part, 1])
-        r_wait(part, 2, 2, far_y1.at[part, 0])
-        add((part, yp, z, slice(None), q[2]), far_y1[part, 0])
-        r_send(part, 2, 3, rows.at[part, yp, z, :, b_cols], far_y2.at[part, 0])
-        r_wait(part, 3, 2, far_y1.at[part, 1])
-        add((part, ym, z, slice(None), q[3]), far_y1[part, 1])
-        r_send(part, 3, 3, rows.at[part, ym, z, :, b_cols], far_y2.at[part, 1])
+        for i in range(4):
+            at_y, at_z = across_y[i], across_z[i]
+            for side, goal in ((0, yp), (1, ym)):
+                r_wait(part, 2 + side, i, near_y1.at[part, side, i])
+                add((part, goal, at_z, slice(None), q[side]), near_y1[part, side, i])
+                r_send(part, 2 + side, 4 + i, rows.at[part, goal, at_z, :, a_cols], near_y2.at[part, side, i])
+            for side, goal in ((0, zp), (1, zm)):
+                r_wait(part, side, i, near_z1.at[part, side, i])
+                add((part, at_y, goal, slice(None), q[2 + side]), near_z1[part, side, i])
+                r_send(part, side, 4 + i, rows.at[part, at_y, goal, :, b_cols], near_z2.at[part, side, i])
+
+    def reduce_3(part, pieces):
+        for i in pieces:
+            at_y, at_z = across_y[i], across_z[i]
+            r_wait(part, 2, 4 + i, near_y2.at[part, 0, i])
+            r_wait(part, 3, 4 + i, near_y2.at[part, 1, i])
+            add((part, y, at_z, slice(None), a_cols), near_y2[part, 0, i], near_y2[part, 1, i])
+            r_wait(part, 0, 4 + i, near_z2.at[part, 0, i])
+            r_wait(part, 1, 4 + i, near_z2.at[part, 1, i])
+            add((part, at_y, z, slice(None), b_cols), near_z2[part, 0, i], near_z2[part, 1, i])
+            if i == 0:
+                for side in range(2):
+                    r_send(part, side, 8, rows.at[part, y, z2, :, q[side]], far_z1.at[part, side])
+                    r_send(part, 2 + side, 8, rows.at[part, y2, z, :, q[2 + side]], far_y1.at[part, side])
+            elif i < 3:
+                side = i - 1
+                r_wait(part, side, 8, far_z1.at[part, side])
+                add((part, y, at_z, slice(None), q[side]), far_z1[part, side])
+                r_send(part, side, 9, rows.at[part, y, at_z, :, a_cols], far_z2.at[part, side])
+                r_wait(part, 2 + side, 8, far_y1.at[part, side])
+                add((part, at_y, z, slice(None), q[2 + side]), far_y1[part, side])
+                r_send(part, 2 + side, 9, rows.at[part, at_y, z, :, b_cols], far_y2.at[part, side])
 
     def back_copy(part, to_core):
-        dest = ((x + chip_offset(part)) % 4) * 2 + to_core
+        dest = ((x + part) % 4) * 2 + to_core
         return pltpu.make_async_remote_copy(
             src_ref=blocks_back.at[part, to_core], dst_ref=returned.at[att],
             send_sem=back_send.at[part, to_core], recv_sem=back_recv.at[att],
@@ -271,21 +267,18 @@
 
     def reduce_5(part):
         for side in range(2):
-            r_wait(part, side, 3, far_z2.at[part, side])
-            r_wait(part, 2 + side, 3, far_y2.at[part, side])
+            r_wait(part, side, 9, far_z2.at[part, side])
+            r_wait(part, 2 + side, 9, far_y2.at[part, side])
         left = rows[part, y, z, :, a_cols].astype(F32) + far_z2[part, 0].astype(F32) + far_z2[part, 1].astype(F32)
         right = rows[part, y, z, :, b_cols].astype(F32) + far_y2[part, 0].astype(F32) + far_y2[part, 1].astype(F32)
         for to_core in range(2):
             lines = slice(8 * to_core, 8 * to_core + 8)
             blocks_back[part, to_core] = jnp.concatenate([left[lines], right[lines]], axis=0).astype(BF16)
 
-        @pl.when(part == 0)
-        def _():
+        if isinstance(part, int) and part == 0:
             back_copy(part, 1 - core).start()
-            returned[att] = blocks_back[0, core]
-
-        @pl.when(part > 0)
-        def _():
+            returned[att] = blocks_back[part, core]
+        else:
             back_copy(part, 0).start()
             back_copy(part, 1).start()
 
@@ -293,21 +286,36 @@
             wait_units(reduce_send.at[part, event], part, units)
 
     gather_own(0)
+    gather_own(1)
 
     @pl.loop(0, 6)
     def _(step):
         gathering = step < 4
         computing = jnp.logical_and(step >= 1, step < 5)
-        reducing = step >= 2
+        sending = jnp.logical_and(step >= 2, step < 5)
+        reducing = step >= 3
         at_c, at_r = step - 1, step - 2
 
+        @pl.when(gathering)
+        def _():
+            gather_a(step)
+
         @pl.when(reducing)
         def _():
-            reduce_2(at_r)
-
-        @pl.when(gathering)
-        def _():
-            gather_a(step)
+            reduce_2(at_r % 3)
+
+        @pl.when(step == 4)
+        def _():
+            reduce_1a(0)
+            reduce_1b(0)
+
+        @pl.when(step >= 4)
+        def _():
+            reduce_5(step - 3)
+
+        @pl.when(computing)
+        def _():
+            gather_e(at_c)
 
         @pl.when(step == 1)
         def _():
@@ -330,13 +338,9 @@
         def _():
             gather_c(step)
 
-        @pl.when(step < 3)
-        def _():
-            gather_own(step + 1)
-
-        @pl.when(reducing)
-        def _():
-            reduce_3(at_r)
+        @pl.when(step < 2)
+        def _():
+            gather_own(step + 2)
 
         @pl.when(computing)
         def _():
@@ -344,30 +348,41 @@
             gather_sent(at_c)
             lower_rows(at_c, 0, 2)
 
+        @pl.when(sending)
+        def _():
+            reduce_1a(at_c)
+
         @pl.when(gathering)
         def _():
             gather_d(step)
 
+        @pl.when(computing)
+        def _():
+            lower_rows(at_c, 2, 4)
+
+        @pl.when(sending)
+        def _():
+            reduce_1b(at_c)
+
         @pl.when(reducing)
         def _():
-            reduce_4(at_r)
-
-        @pl.when(computing)
-        def _():
-            lower_rows(at_c, 2, 4)
-
-        @pl.when(gathering)
-        def _():
-            gather_e(step)
-
-        @pl.when(computing)
-        def _():
-            reduce_1(at_c)
+            reduce_3(at_r, (0,))
+
+        @pl.when(step == 4)
+        def _():
+            reduce_2(3)
 
         @pl.when(reducing)
         def _():
-            reduce_5(at_r)
-
+            reduce_3(at_r, (1, 2, 3))
+
+        @pl.when(step == 5)
+        def _():
+            reduce_3(0, (0,))
+
+    reduce_3(0, (1, 2, 3))
+    reduce_5(3)
+    reduce_5(0)
     in_copy(0, 1 - core).wait_send()
     back_copy(0, 1 - core).wait_send()
     for part in range(1, 4):
@@ -405,8 +420,8 @@
             vmem((4, 2, 16, half), BF16),
             vmem((8, 16, half), BF16),
             vmem((4, 4, 4, 16, width), BF16),
-            vmem((256, units), F32),
-            vmem((256, units), F32),
+            vmem((units, 256), F32),
+            vmem((units, 256), F32),
             vmem((256, units), BF16),
             vmem((4, 2, 4, 16, quarter), BF16),
             vmem((4, 2, 4, 16, quarter), BF16),
@@ -424,7 +439,7 @@
             dma((4, 9)),
             dma((4, 4, 9)),
             dma((4, 4)),
-            dma((4, 4, 4)),
+            dma((4, 4, 10)),
         ],
         compiler_params=pltpu.CompilerParams(
             collective_id=0, has_side_effects=True, vmem_limit_bytes=62 * 1024 * 1024

time: 194 us -> 175 us (0.902)
  Pallas kernels: 192 us -> 173 us
    pallas_call x1, Pallas kernels: 192 us -> 173 us  [per_device(): pl.pallas_call(ffn_kernel, out_shape=jax.ShapeDtypeStruct((row_count, wid...]
where the time goes in v3:
time: 175 us
  Pallas kernels  173 us (99%)
  local copies, waits for them, and re-layouts  1.82 us (1%)
    pallas_call x1, Pallas kernels, per_device(): pl.pallas_call(ffn_kernel, out_shape=jax.ShapeDtypeStruct((row_count, wid...  173 us

profile of v3, /device:TPU:1, one launch (start us, length us, event | category | flops | bytes accessed | tf_op | source)
XLA Modules:
  0.0 175.1 jit_solution(11609657176616683281)
XLA Ops:
  0.0 173.3 %shard_map.64 = bf16[32,7168]{1,0:T(8,128)(2,1)} custom-call(bf16[32,7168]{1,0:T(8,128)(2,1)} %hidden.1, s32[1,32]{1,0:T(1,128)} %bitcast.7, f32[1,7168]{1,0:T(1,128)} %bitcast.6, bf16[1,576,7168]{2,1,0:T(8,128)(2,1)} %bitcast.4, bf16[1,576,7168]{2,1,0:T(8,128)(2,1)} %bitcast.5, bf16[1,576,7168]{2,1,0:T(8,128)(2,1)} %down_hbm.1), custom_call_target="tpu_custom_call" | custom-call | tf_op jit(solution)/shard_map/pallas_call | solution.py:409
  173.3 1.8 %copy.8 = bf16[32,7168]{1,0:T(8,128)(2,1)} copy(bf16[32,7168]{1,0:T(8,128)(2,1)} %shard_map.64) | data formatting | bytes 917504

commit v4 on v3

--- a/solution.py
+++ b/solution.py
@@ -12,11 +12,31 @@
 LAST = (((1,), (1,)), ((), ()))
 
 
+RAW = 4
+
+
+def chip_offset(part):
+    return part + part // 2 - 2 * (part // 3)
+
+
+def raw_columns(width):
+    return width // 4
+
+
+def halves(width):
+    half = width // 2
+    more = (half // 128 + 1) // 2 * 128
+    less = half - more
+    quarters = [pl.ds(0, more), pl.ds(more, less), pl.ds(half, less), pl.ds(half + less, more)]
+    return pl.ds(0, width), pl.ds(0, half), pl.ds(half, half), quarters
+
+
 def ffn_kernel(
     hidden, route, gain, gate_hbm, up_hbm, down_hbm, out,
-    w_gate, w_up, w_down, blocks_out, blocks_in, blocks_back, returned, rows, gate_sum, up_sum, mid,
+    w_gate, w_up, w_down, blocks_out, blocks_in, blocks_back, returned, rows, raw, slots,
+    gate_sum, up_sum, mid,
     near_y1, near_z1, near_y2, near_z2, far_z1, far_y1, far_z2, far_y2,
-    w_sem, in_send, in_recv, back_send, back_recv, gather_send, gather_recv, reduce_send, reduce_recv,
+    w_sem, in_send, in_recv, shift_send, shift_recv, home_sem, back_send, back_recv, gather_send, gather_recv, reduce_send, reduce_recv,
 ):
     att, ffn = lax.axis_index("att"), lax.axis_index("ffn")
     x, core = att // 2, att % 2
@@ -27,6 +47,10 @@
     half, quarter = width // 2, width // 4
     a_cols, b_cols = pl.ds(0, half), pl.ds(half, half)
     q = [pl.ds(i * quarter, quarter) for i in range(4)]
+    extra = raw_columns(width)
+    split = width - extra
+    g_half, x_half = split // 2, extra // 2
+    slot_geometry, raw_geometry = halves(split), halves(2 * extra + 256)
     z_plus, z_minus, y_plus, y_minus = (att, y * 4 + zp), (att, y * 4 + zm), (att, yp * 4 + z), (att, ym * 4 + z)
     ALL = pl.ds(0, 4)
 
@@ -55,33 +79,38 @@
     line = lax.broadcasted_iota(jnp.int32, (128, 32), 0)
     table_a = (line == place).astype(F32).astype(BF16)
     table_b = (line == place + 8).astype(F32).astype(BF16)
-    placed = jnp.dot(table_a, normed[:, :half], preferred_element_type=F32)
-    placed = placed + jnp.dot(table_b, normed[:, half:], preferred_element_type=F32)
-    blocks_out[...] = placed.astype(BF16).reshape(8, 16, half)
+    placed = jnp.dot(table_a, normed[:, :g_half], preferred_element_type=F32)
+    placed = placed + jnp.dot(table_b, normed[:, g_half:split], preferred_element_type=F32)
+    blocks_out[...] = placed.astype(BF16).reshape(8, 16, g_half)
+    number = jnp.broadcast_to(place.astype(F32), (128, 32)).T.astype(BF16)
+    for i in range(2):
+        lines = slice(16 * i, 16 * i + 16)
+        raw[y, z, :, extra * i : extra * (i + 1)] = normed[lines, split:]
+        raw[y, z, :, 2 * extra + 128 * i : 2 * extra + 128 * (i + 1)] = number[lines]
 
     pl.semaphore_wait(barrier, 11)
 
     def in_copy(part, to_core):
-        dest = ((x + 4 - part) % 4) * 2 + to_core
+        dest = ((x + 4 - chip_offset(part)) % 4) * 2 + to_core
         return pltpu.make_async_remote_copy(
             src_ref=blocks_out.at[dest], dst_ref=blocks_in.at[part, core],
             send_sem=in_send.at[part, to_core], recv_sem=in_recv.at[part, core],
             device_id=(dest, ffn), device_id_type=MESH,
         )
 
-    in_copy(0, 1 - core).start()
-    for part in range(1, 4):
-        for to_core in range(2):
-            in_copy(part, to_core).start()
-    blocks_in[0, core] = blocks_out[att]
-
     def wait_in(part, from_core):
         pltpu.make_async_copy(blocks_out.at[0], blocks_in.at[part, from_core], in_recv.at[part, from_core]).wait()
 
     LINK = {0: z_plus, 1: z_minus, 2: y_plus, 3: y_minus}
 
+    def geometry(part):
+        return raw_geometry if part is RAW else slot_geometry
+
+    def unit(part, at_y, at_z, cols):
+        return raw.at[at_y, at_z, :, cols] if part is RAW else rows.at[part, at_y, at_z, :, cols]
+
     def g_send(part, link, event, at_y, at_z, cols):
-        piece = rows.at[part, at_y, at_z, :, cols]
+        piece = unit(part, at_y, at_z, cols)
         pltpu.make_async_remote_copy(
             src_ref=piece, dst_ref=piece,
             send_sem=gather_send.at[part, event], recv_sem=gather_recv.at[part, link, event],
@@ -89,10 +118,8 @@
         ).start()
 
     def g_wait(part, link, event, cols):
-        piece = rows.at[part, 0, 0, :, cols]
+        piece = unit(part, 0, 0, cols)
         pltpu.make_async_copy(piece, piece, gather_recv.at[part, link, event]).wait()
-
-    whole = pl.ds(0, width)
 
     def gather_own(part):
         @pl.when(part == 0)
@@ -105,46 +132,53 @@
             wait_in(part, 1)
 
         first, second = blocks_in[part, 0].astype(F32), blocks_in[part, 1].astype(F32)
-        rows[part, y, z, :, a_cols] = jnp.concatenate([first[:8], second[:8]], axis=0).astype(BF16)
-        rows[part, y, z, :, b_cols] = jnp.concatenate([first[8:], second[8:]], axis=0).astype(BF16)
+        _, ga_cols, gb_cols, _ = slot_geometry
+        rows[part, y, z, :, ga_cols] = jnp.concatenate([first[:8], second[:8]], axis=0).astype(BF16)
+        rows[part, y, z, :, gb_cols] = jnp.concatenate([first[8:], second[8:]], axis=0).astype(BF16)
+        send_own(part)
+
+    def send_own(part):
         for link in range(4):
-            g_send(part, link, 0, y, z, whole)
+            g_send(part, link, 0, y, z, geometry(part)[0])
 
     def gather_a(part):
+        whole, ga_cols, gb_cols, g = geometry(part)
         for link in range(4):
             g_wait(part, link, 0, whole)
-        g_send(part, 0, 1, y, zm, q[0])
-        g_send(part, 1, 1, y, zp, q[1])
-        g_send(part, 2, 1, ym, z, q[2])
-        g_send(part, 3, 1, yp, z, q[3])
+        g_send(part, 0, 1, y, zm, g[0])
+        g_send(part, 1, 1, y, zp, g[1])
+        g_send(part, 2, 1, ym, z, g[2])
+        g_send(part, 3, 1, yp, z, g[3])
         for link in (2, 3):
-            g_send(part, link, 2, y, zm, a_cols)
+            g_send(part, link, 2, y, zm, ga_cols)
         for link in (0, 1):
-            g_send(part, link, 2, ym, z, b_cols)
+            g_send(part, link, 2, ym, z, gb_cols)
         for link in (2, 3):
-            g_send(part, link, 3, y, zp, a_cols)
+            g_send(part, link, 3, y, zp, ga_cols)
         for link in (0, 1):
-            g_send(part, link, 3, yp, z, b_cols)
-        g_send(part, 0, 5, y, zm, q[2])
-        g_send(part, 1, 5, y, zp, q[3])
-        g_send(part, 2, 5, ym, z, q[0])
-        g_send(part, 3, 5, yp, z, q[1])
+            g_send(part, link, 3, yp, z, gb_cols)
+        g_send(part, 0, 5, y, zm, g[2])
+        g_send(part, 1, 5, y, zp, g[3])
+        g_send(part, 2, 5, ym, z, g[0])
+        g_send(part, 3, 5, yp, z, g[1])
 
     def gather_b(part):
+        _, ga_cols, gb_cols, g = geometry(part)
         for link in range(4):
-            g_wait(part, link, 1, q[0])
+            g_wait(part, link, 1, g[link])
         for link in (2, 3):
-            g_send(part, link, 4, y, z2, a_cols)
+            g_send(part, link, 4, y, z2, ga_cols)
         for link in (0, 1):
-            g_send(part, link, 4, y2, z, b_cols)
+            g_send(part, link, 4, y2, z, gb_cols)
 
     def gather_on(part, event, of_y, of_z):
+        _, ga_cols, _, g = geometry(part)
         for link in range(4):
-            g_wait(part, link, event, a_cols)
-        g_send(part, 0, event + 4, of_y, zm, q[2])
-        g_send(part, 1, event + 4, of_y, zp, q[3])
-        g_send(part, 2, event + 4, ym, of_z, q[0])
-        g_send(part, 3, event + 4, yp, of_z, q[1])
+            g_wait(part, link, event, ga_cols)
+        g_send(part, 0, event + 4, of_y, zm, g[2])
+        g_send(part, 1, event + 4, of_y, zp, g[3])
+        g_send(part, 2, event + 4, ym, of_z, g[0])
+        g_send(part, 3, event + 4, yp, of_z, g[1])
 
     def gather_c(part):
         gather_on(part, 2, ym, zm)
@@ -154,9 +188,10 @@
         gather_on(part, 4, y2, z2)
 
     def gather_e(part):
+        g = geometry(part)[3]
         for event in range(5, 9):
             for link in range(4):
-                g_wait(part, link, event, q[0])
+                g_wait(part, link, event, g[(link + 2) % 4])
 
     def wait_units(sem, part, units):
         piece = rows.at[part, 0, pl.ds(0, units)] if units <= 4 else rows.at[part, pl.ds(0, units // 4)]
@@ -164,7 +199,73 @@
 
     def gather_sent(part):
         for event, units in enumerate((4, 1, 2, 2, 2, 1, 1, 1, 1)):
-            wait_units(gather_send.at[part, event], part, units)
+            if part is RAW:
+                piece = raw.at[0, pl.ds(0, units)]
+            else:
+                piece = rows.at[part, 0, pl.ds(0, units), :, slot_geometry[0]]
+            pltpu.make_async_copy(piece, piece, gather_send.at[part, event]).wait()
+
+    def fill_slots():
+        lane = lax.broadcasted_iota(jnp.int32, (32, 128), 1)
+
+        @pl.loop(0, 16)
+        def _(i):
+            of_y, of_z = i // 4, i % 4
+            where = jnp.concatenate([raw[of_y, of_z, :, pl.ds(2 * extra + 128 * j, 128)] for j in (0, 1)], axis=0)
+            where = where.astype(F32).astype(jnp.int32)
+            table = jnp.concatenate([(lane == where).astype(F32), (lane == where + 8).astype(F32)], axis=0).astype(BF16)
+            lines = [raw[of_y, of_z, :, pl.ds(extra * j + x_half * k, x_half)] for k in (0, 1) for j in (0, 1)]
+            filled = lax.dot_general(table, jnp.concatenate(lines, axis=0), FIRST, preferred_element_type=F32)
+            slots[:, of_y, of_z] = filled.astype(BF16).reshape(8, 16, x_half)
+
+    def shifted(part, from_core):
+        cols = pl.ds(pl.multiple_of(split + from_core * x_half, 128), x_half)
+        return rows.at[part, :, :, :, cols]
+
+    def shift_copy(part, to_core):
+        dest = ((x + 4 - chip_offset(part)) % 4) * 2 + to_core
+        return pltpu.make_async_remote_copy(
+            src_ref=slots.at[dest], dst_ref=shifted(part, core),
+            send_sem=shift_send.at[part, to_core], recv_sem=shift_recv.at[part, core],
+            device_id=(dest, ffn), device_id_type=MESH,
+        )
+
+    def shift_home():
+        return pltpu.make_async_copy(slots.at[att], shifted(0, core), home_sem)
+
+    def shift(part):
+        if part == 0:
+            shift_home().start()
+            shift_copy(0, 1 - core).start()
+        else:
+            shift_copy(part, 0).start()
+            shift_copy(part, 1).start()
+
+    def wait_shift(part, from_core):
+        pltpu.make_async_copy(slots.at[0], shifted(part, from_core), shift_recv.at[part, from_core]).wait()
+
+    def complete(part):
+        @pl.when(part == 0)
+        def _():
+            shift_home().wait()
+            wait_shift(0, 1 - core)
+
+        @pl.when(part > 0)
+        def _():
+            wait_shift(part, 0)
+            wait_shift(part, 1)
+
+        @pl.loop(0, 16)
+        def _(i):
+            of_y, of_z = i // 4, i % 4
+            first = rows[part, of_y, of_z, :, split : split + x_half].astype(F32)
+            second = rows[part, of_y, of_z, :, split + x_half :].astype(F32)
+            rows[part, of_y, of_z, :, split : split + x_half] = (
+                jnp.concatenate([first[:8], second[:8]], axis=0).astype(BF16)
+            )
+            rows[part, of_y, of_z, :, split + x_half :] = (
+                jnp.concatenate([first[8:], second[8:]], axis=0).astype(BF16)
+            )
 
     def project(part, lower, upper):
         @pl.loop(lower, upper)
@@ -213,52 +314,55 @@
 
     across_z, across_y = (z2, zp, zm, z), (y2, yp, ym, y)
 
+    def landing(part):
+        return part * 2 // 3
+
     def reduce_1a(part):
         for i in range(4):
-            r_send(part, 2, i, rows.at[part, y2, across_z[i], :, q[0]], near_y1.at[part, 0, i])
-            r_send(part, 3, i, rows.at[part, y2, across_z[i], :, q[1]], near_y1.at[part, 1, i])
+            r_send(part, 2, i, rows.at[part, y2, across_z[i], :, q[0]], near_y1.at[landing(part), 0, i])
+            r_send(part, 3, i, rows.at[part, y2, across_z[i], :, q[1]], near_y1.at[landing(part), 1, i])
 
     def reduce_1b(part):
         for i in range(4):
-            r_send(part, 0, i, rows.at[part, across_y[i], z2, :, q[2]], near_z1.at[part, 0, i])
-            r_send(part, 1, i, rows.at[part, across_y[i], z2, :, q[3]], near_z1.at[part, 1, i])
+            r_send(part, 0, i, rows.at[part, across_y[i], z2, :, q[2]], near_z1.at[landing(part), 0, i])
+            r_send(part, 1, i, rows.at[part, across_y[i], z2, :, q[3]], near_z1.at[landing(part), 1, i])
 
     def reduce_2(part):
         for i in range(4):
             at_y, at_z = across_y[i], across_z[i]
             for side, goal in ((0, yp), (1, ym)):
-                r_wait(part, 2 + side, i, near_y1.at[part, side, i])
-                add((part, goal, at_z, slice(None), q[side]), near_y1[part, side, i])
-                r_send(part, 2 + side, 4 + i, rows.at[part, goal, at_z, :, a_cols], near_y2.at[part, side, i])
+                r_wait(part, 2 + side, i, near_y1.at[landing(part), side, i])
+                add((part, goal, at_z, slice(None), q[side]), near_y1[landing(part), side, i])
+                r_send(part, 2 + side, 4 + i, rows.at[part, goal, at_z, :, a_cols], near_y2.at[landing(part), side, i])
             for side, goal in ((0, zp), (1, zm)):
-                r_wait(part, side, i, near_z1.at[part, side, i])
-                add((part, at_y, goal, slice(None), q[2 + side]), near_z1[part, side, i])
-                r_send(part, side, 4 + i, rows.at[part, at_y, goal, :, b_cols], near_z2.at[part, side, i])
+                r_wait(part, side, i, near_z1.at[landing(part), side, i])
+                add((part, at_y, goal, slice(None), q[2 + side]), near_z1[landing(part), side, i])
+                r_send(part, side, 4 + i, rows.at[part, at_y, goal, :, b_cols], near_z2.at[landing(part), side, i])
 
     def reduce_3(part, pieces):
         for i in pieces:
             at_y, at_z = across_y[i], across_z[i]
-            r_wait(part, 2, 4 + i, near_y2.at[part, 0, i])
-            r_wait(part, 3, 4 + i, near_y2.at[part, 1, i])
-            add((part, y, at_z, slice(None), a_cols), near_y2[part, 0, i], near_y2[part, 1, i])
-            r_wait(part, 0, 4 + i, near_z2.at[part, 0, i])
-            r_wait(part, 1, 4 + i, near_z2.at[part, 1, i])
-            add((part, at_y, z, slice(None), b_cols), near_z2[part, 0, i], near_z2[part, 1, i])
+            r_wait(part, 2, 4 + i, near_y2.at[landing(part), 0, i])
+            r_wait(part, 3, 4 + i, near_y2.at[landing(part), 1, i])
+            add((part, y, at_z, slice(None), a_cols), near_y2[landing(part), 0, i], near_y2[landing(part), 1, i])
+            r_wait(part, 0, 4 + i, near_z2.at[landing(part), 0, i])
+            r_wait(part, 1, 4 + i, near_z2.at[landing(part), 1, i])
+            add((part, at_y, z, slice(None), b_cols), near_z2[landing(part), 0, i], near_z2[landing(part), 1, i])
             if i == 0:
                 for side in range(2):
-                    r_send(part, side, 8, rows.at[part, y, z2, :, q[side]], far_z1.at[part, side])
-                    r_send(part, 2 + side, 8, rows.at[part, y2, z, :, q[2 + side]], far_y1.at[part, side])
+                    r_send(part, side, 8, rows.at[part, y, z2, :, q[side]], far_z1.at[landing(part), side])
+                    r_send(part, 2 + side, 8, rows.at[part, y2, z, :, q[2 + side]], far_y1.at[landing(part), side])
             elif i < 3:
                 side = i - 1
-                r_wait(part, side, 8, far_z1.at[part, side])
-                add((part, y, at_z, slice(None), q[side]), far_z1[part, side])
-                r_send(part, side, 9, rows.at[part, y, at_z, :, a_cols], far_z2.at[part, side])
-                r_wait(part, 2 + side, 8, far_y1.at[part, side])
-                add((part, at_y, z, slice(None), q[2 + side]), far_y1[part, side])
-                r_send(part, 2 + side, 9, rows.at[part, at_y, z, :, b_cols], far_y2.at[part, side])
+                r_wait(part, side, 8, far_z1.at[landing(part), side])
+                add((part, y, at_z, slice(None), q[side]), far_z1[landing(part), side])
+                r_send(part, side, 9, rows.at[part, y, at_z, :, a_cols], far_z2.at[landing(part), side])
+                r_wait(part, 2 + side, 8, far_y1.at[landing(part), side])
+                add((part, at_y, z, slice(None), q[2 + side]), far_y1[landing(part), side])
+                r_send(part, 2 + side, 9, rows.at[part, at_y, z, :, b_cols], far_y2.at[landing(part), side])
 
     def back_copy(part, to_core):
-        dest = ((x + part) % 4) * 2 + to_core
+        dest = ((x + chip_offset(part)) % 4) * 2 + to_core
         return pltpu.make_async_remote_copy(
             src_ref=blocks_back.at[part, to_core], dst_ref=returned.at[att],
             send_sem=back_send.at[part, to_core], recv_sem=back_recv.at[att],
@@ -267,10 +371,10 @@
 
     def reduce_5(part):
         for side in range(2):
-            r_wait(part, side, 9, far_z2.at[part, side])
-            r_wait(part, 2 + side, 9, far_y2.at[part, side])
-        left = rows[part, y, z, :, a_cols].astype(F32) + far_z2[part, 0].astype(F32) + far_z2[part, 1].astype(F32)
-        right = rows[part, y, z, :, b_cols].astype(F32) + far_y2[part, 0].astype(F32) + far_y2[part, 1].astype(F32)
+            r_wait(part, side, 9, far_z2.at[landing(part), side])
+            r_wait(part, 2 + side, 9, far_y2.at[landing(part), side])
+        left = rows[part, y, z, :, a_cols].astype(F32) + far_z2[landing(part), 0].astype(F32) + far_z2[landing(part), 1].astype(F32)
+        right = rows[part, y, z, :, b_cols].astype(F32) + far_y2[landing(part), 0].astype(F32) + far_y2[landing(part), 1].astype(F32)
         for to_core in range(2):
             lines = slice(8 * to_core, 8 * to_core + 8)
             blocks_back[part, to_core] = jnp.concatenate([left[lines], right[lines]], axis=0).astype(BF16)
@@ -285,8 +389,18 @@
         for event, units in enumerate((4, 8, 1, 2)):
             wait_units(reduce_send.at[part, event], part, units)
 
+    send_own(RAW)
+    in_copy(0, 1 - core).start()
+    for part in range(1, 4):
+        for to_core in range(2):
+            in_copy(part, to_core).start()
+    blocks_in[0, core] = blocks_out[att]
     gather_own(0)
+    gather_a(RAW)
+    gather_b(RAW)
+    gather_c(RAW)
     gather_own(1)
+    gather_d(RAW)
 
     @pl.loop(0, 6)
     def _(step):
@@ -296,6 +410,10 @@
         reducing = step >= 3
         at_c, at_r = step - 1, step - 2
 
+        @pl.when(step == 2)
+        def _():
+            shift(3)
+
         @pl.when(gathering)
         def _():
             gather_a(step)
@@ -317,6 +435,13 @@
         def _():
             gather_e(at_c)
 
+        @pl.when(step == 0)
+        def _():
+            gather_e(RAW)
+            fill_slots()
+            for part in range(3):
+                shift(part)
+
         @pl.when(step == 1)
         def _():
             for load in loads:
@@ -324,6 +449,7 @@
 
         @pl.when(computing)
         def _():
+            complete(at_c)
             project(at_c, 0, 2)
 
         @pl.when(gathering)
@@ -383,15 +509,18 @@
     reduce_3(0, (1, 2, 3))
     reduce_5(3)
     reduce_5(0)
+    gather_sent(RAW)
+    shift_copy(0, 1 - core).wait_send()
     in_copy(0, 1 - core).wait_send()
     back_copy(0, 1 - core).wait_send()
     for part in range(1, 4):
         for to_core in range(2):
+            shift_copy(part, to_core).wait_send()
             in_copy(part, to_core).wait_send()
             back_copy(part, to_core).wait_send()
     for step in range(1, 8):
         source = (att + step) % 8
-        pltpu.make_async_copy(blocks_out.at[0], returned.at[source], back_recv.at[source]).wait()
+        pltpu.make_async_copy(blocks_back.at[0, 0], returned.at[source], back_recv.at[source]).wait()
     lines = returned[...].reshape(128, half)
     out[:, :half] = (
         hidden[:, :half].astype(F32) + lax.dot_general(table_a, lines, FIRST, preferred_element_type=F32)
@@ -405,6 +534,8 @@
     row_count, width = hidden.shape
     units = gate_weight.shape[2]
     half, quarter = width // 2, width // 4
+    extra = raw_columns(width)
+    split = width - extra
     vmem, dma = pltpu.VMEM, pltpu.SemaphoreType.DMA
     return pl.pallas_call(
         ffn_kernel,
@@ -415,34 +546,39 @@
             vmem((units, width), BF16),
             vmem((units, width), BF16),
             vmem((units, width), BF16),
-            vmem((8, 16, half), BF16),
-            vmem((4, 2, 16, half), BF16),
+            vmem((8, 16, split // 2), BF16),
+            vmem((4, 2, 16, split // 2), BF16),
             vmem((4, 2, 16, half), BF16),
             vmem((8, 16, half), BF16),
             vmem((4, 4, 4, 16, width), BF16),
+            vmem((4, 4, 16, 2 * extra + 256), BF16),
+            vmem((8, 4, 4, 16, extra // 2), BF16),
             vmem((units, 256), F32),
             vmem((units, 256), F32),
             vmem((256, units), BF16),
-            vmem((4, 2, 4, 16, quarter), BF16),
-            vmem((4, 2, 4, 16, quarter), BF16),
-            vmem((4, 2, 4, 16, half), BF16),
-            vmem((4, 2, 4, 16, half), BF16),
-            vmem((4, 2, 16, quarter), BF16),
-            vmem((4, 2, 16, quarter), BF16),
-            vmem((4, 2, 16, half), BF16),
-            vmem((4, 2, 16, half), BF16),
+            vmem((3, 2, 4, 16, quarter), BF16),
+            vmem((3, 2, 4, 16, quarter), BF16),
+            vmem((3, 2, 4, 16, half), BF16),
+            vmem((3, 2, 4, 16, half), BF16),
+            vmem((3, 2, 16, quarter), BF16),
+            vmem((3, 2, 16, quarter), BF16),
+            vmem((3, 2, 16, half), BF16),
+            vmem((3, 2, 16, half), BF16),
             dma((3,)),
             dma((4, 2)),
             dma((4, 2)),
             dma((4, 2)),
+            dma((4, 2)),
+            dma,
+            dma((4, 2)),
             dma((8,)),
-            dma((4, 9)),
-            dma((4, 4, 9)),
+            dma((5, 9)),
+            dma((5, 4, 9)),
             dma((4, 4)),
             dma((4, 4, 10)),
         ],
         compiler_params=pltpu.CompilerParams(
-            collective_id=0, has_side_effects=True, vmem_limit_bytes=62 * 1024 * 1024
+            collective_id=0, has_side_effects=True, vmem_limit_bytes=63 * 1024 * 1024
         ),
     )(
         hidden, route.reshape(1, row_count), norm_gain.reshape(1, width),

time: 175 us -> 168 us (0.960)
  Pallas kernels: 173 us -> 166 us
    pallas_call x1, Pallas kernels: 173 us -> 166 us  [per_device(): pl.pallas_call(ffn_kernel, out_shape=jax.ShapeDtypeStruct((row_count, wid...]
where the time goes in v4:
time: 168 us
  Pallas kernels  166 us (99%)
  local copies, waits for them, and re-layouts  1.82 us (1%)
    pallas_call x1, Pallas kernels, per_device(): pl.pallas_call(ffn_kernel, out_shape=jax.ShapeDtypeStruct((row_count, wid...  166 us

profile of v4, /device:TPU:1, one launch (start us, length us, event | category | flops | bytes accessed | tf_op | source)
XLA Modules:
  0.0 167.8 jit_solution(4360036649102544110)
XLA Ops:
  0.0 166.0 %shard_map.64 = bf16[32,7168]{1,0:T(8,128)(2,1)} custom-call(bf16[32,7168]{1,0:T(8,128)(2,1)} %hidden.1, s32[1,32]{1,0:T(1,128)} %bitcast.7, f32[1,7168]{1,0:T(1,128)} %bitcast.6, bf16[1,576,7168]{2,1,0:T(8,128)(2,1)} %bitcast.4, bf16[1,576,7168]{2,1,0:T(8,128)(2,1)} %bitcast.5, bf16[1,576,7168]{2,1,0:T(8,128)(2,1)} %down_hbm.1), custom_call_target="tpu_custom_call" | custom-call | tf_op jit(solution)/shard_map/pallas_call | solution.py:540
  166.0 1.8 %copy.8 = bf16[32,7168]{1,0:T(8,128)(2,1)} copy(bf16[32,7168]{1,0:T(8,128)(2,1)} %shard_map.64) | data formatting | bytes 917504

commit v5 on v4

--- a/solution.py
+++ b/solution.py
@@ -1,3 +1,5 @@
+import functools
+
 import jax
 import jax.numpy as jnp
 from jax import lax
@@ -14,6 +16,14 @@
 
 RAW = 4
 
+ORDER = (
+    4, 88, 8, 12, 1, 92, 2, 16, 96, 20, 5, 9, 24, 13, 17, 3, 28, 21, 6, 32,
+    36, 40, 10, 14, 7, 100, 25, 29, 18, 22, 33, 11, 37, 45, 41, 49, 53, 15, 19, 26,
+    23, 57, 61, 30, 65, 69, 34, 38, 46, 42, 50, 27, 54, 73, 77, 58, 31, 62, 66, 44,
+    35, 70, 39, 47, 81, 48, 43, 51, 85, 55, 59, 63, 74, 67, 71, 78, 52, 56, 60, 64,
+    68, 75, 82, 86, 79, 72, 76, 83, 80, 87, 84,
+)
+
 
 def chip_offset(part):
     return part + part // 2 - 2 * (part // 3)
@@ -33,7 +43,7 @@
 
 def ffn_kernel(
     hidden, route, gain, gate_hbm, up_hbm, down_hbm, out,
-    w_gate, w_up, w_down, blocks_out, blocks_in, blocks_back, returned, rows, raw, slots,
+    w_gate, w_up, w_down, blocks_out, blocks_back, returned, rows, raw, slots,
     gate_sum, up_sum, mid,
     near_y1, near_z1, near_y2, near_z2, far_z1, far_y1, far_z2, far_y2,
     w_sem, in_send, in_recv, shift_send, shift_recv, home_sem, back_send, back_recv, gather_send, gather_recv, reduce_send, reduce_recv,
@@ -90,16 +100,19 @@
 
     pl.semaphore_wait(barrier, 11)
 
+    def arrival(part, from_core):
+        return rows.at[part, y, z, :, pl.ds(pl.multiple_of(from_core * g_half, 128), g_half)]
+
     def in_copy(part, to_core):
         dest = ((x + 4 - chip_offset(part)) % 4) * 2 + to_core
         return pltpu.make_async_remote_copy(
-            src_ref=blocks_out.at[dest], dst_ref=blocks_in.at[part, core],
+            src_ref=blocks_out.at[dest], dst_ref=arrival(part, core),
             send_sem=in_send.at[part, to_core], recv_sem=in_recv.at[part, core],
             device_id=(dest, ffn), device_id_type=MESH,
         )
 
     def wait_in(part, from_core):
-        pltpu.make_async_copy(blocks_out.at[0], blocks_in.at[part, from_core], in_recv.at[part, from_core]).wait()
+        pltpu.make_async_copy(blocks_out.at[0], arrival(part, from_core), in_recv.at[part, from_core]).wait()
 
     LINK = {0: z_plus, 1: z_minus, 2: y_plus, 3: y_minus}
 
@@ -131,8 +144,8 @@
             wait_in(part, 0)
             wait_in(part, 1)
 
-        first, second = blocks_in[part, 0].astype(F32), blocks_in[part, 1].astype(F32)
         _, ga_cols, gb_cols, _ = slot_geometry
+        first, second = rows[part, y, z, :, ga_cols].astype(F32), rows[part, y, z, :, gb_cols].astype(F32)
         rows[part, y, z, :, ga_cols] = jnp.concatenate([first[:8], second[:8]], axis=0).astype(BF16)
         rows[part, y, z, :, gb_cols] = jnp.concatenate([first[8:], second[8:]], axis=0).astype(BF16)
         send_own(part)
@@ -182,9 +195,11 @@
 
     def gather_c(part):
         gather_on(part, 2, ym, zm)
+
+    def gather_d(part):
         gather_on(part, 3, yp, zp)
 
-    def gather_d(part):
+    def gather_f(part):
         gather_on(part, 4, y2, z2)
 
     def gather_e(part):
@@ -267,8 +282,8 @@
                 jnp.concatenate([first[8:], second[8:]], axis=0).astype(BF16)
             )
 
-    def project(part, lower, upper):
-        @pl.loop(lower, upper)
+    def project(part, lower):
+        @pl.loop(lower, lower + 2)
         def _(i):
             cols = pl.ds(pl.multiple_of(i * quarter, quarter), quarter)
             block = rows[part, :, :, :, cols].reshape(256, quarter)
@@ -289,8 +304,8 @@
         gate = gate_sum[...]
         mid[...] = (gate / (1.0 + jnp.exp(-gate)) * up_sum[...]).T.astype(BF16)
 
-    def lower_rows(part, lower, upper):
-        @pl.loop(lower, upper)
+    def lower_rows(part, lower):
+        @pl.loop(lower, lower + 2)
         def _(i):
             cols = pl.ds(pl.multiple_of(i * quarter, quarter), quarter)
             partial = jnp.dot(mid[...], w_down[:, cols], preferred_element_type=F32)
@@ -327,8 +342,8 @@
             r_send(part, 0, i, rows.at[part, across_y[i], z2, :, q[2]], near_z1.at[landing(part), 0, i])
             r_send(part, 1, i, rows.at[part, across_y[i], z2, :, q[3]], near_z1.at[landing(part), 1, i])
 
-    def reduce_2(part):
-        for i in range(4):
+    def reduce_2(part, pieces):
+        for i in pieces:
             at_y, at_z = across_y[i], across_z[i]
             for side, goal in ((0, yp), (1, ym)):
                 r_wait(part, 2 + side, i, near_y1.at[landing(part), side, i])
@@ -379,10 +394,13 @@
             lines = slice(8 * to_core, 8 * to_core + 8)
             blocks_back[part, to_core] = jnp.concatenate([left[lines], right[lines]], axis=0).astype(BF16)
 
-        if isinstance(part, int) and part == 0:
+        @pl.when(part == 0)
+        def _():
             back_copy(part, 1 - core).start()
             returned[att] = blocks_back[part, core]
-        else:
+
+        @pl.when(part > 0)
+        def _():
             back_copy(part, 0).start()
             back_copy(part, 1).start()
 
@@ -394,121 +412,69 @@
     for part in range(1, 4):
         for to_core in range(2):
             in_copy(part, to_core).start()
-    blocks_in[0, core] = blocks_out[att]
+    rows[0, y, z, :, pl.ds(pl.multiple_of(core * g_half, 128), g_half)] = blocks_out[att]
     gather_own(0)
     gather_a(RAW)
     gather_b(RAW)
     gather_c(RAW)
-    gather_own(1)
     gather_d(RAW)
 
-    @pl.loop(0, 6)
+    def products(part, second):
+        @pl.when(jnp.logical_not(second))
+        def _():
+            complete(part)
+
+        project(part, jnp.where(second, 2, 0))
+
+    def lowering(part, second):
+        @pl.when(jnp.logical_not(second))
+        def _():
+            activate()
+            gather_sent(part)
+
+        lower_rows(part, jnp.where(second, 2, 0))
+
+    def spread(part):
+        for load in loads:
+            load.wait()
+        fill_slots()
+        for part in range(3):
+            shift(part)
+
+    steps = [
+        gather_own, gather_a, gather_b, gather_c, gather_d, gather_f, gather_e,
+        products, products, lowering, lowering, reduce_1a, reduce_1b,
+        *[functools.partial(reduce_2, pieces=(i,)) for i in range(4)],
+        *[functools.partial(reduce_3, pieces=(i,)) for i in range(4)],
+        reduce_5,
+        lambda part: gather_f(RAW), lambda part: gather_e(RAW), spread, lambda part: shift(3),
+    ]
+
+    def take(kind, part, low, high):
+        if high - low == 1:
+            steps[low](part)
+        elif steps[low] is steps[high - 1]:
+            steps[low](part, kind > low)
+        else:
+            middle = (low + high) // 2
+            if steps[middle] is steps[middle - 1]:
+                middle += 1
+            lax.cond(
+                kind < middle, lambda: take(kind, part, low, middle), lambda: take(kind, part, middle, high)
+            )
+
+    per_word = 4
+    words = [sum(code << (7 * k) for k, code in enumerate(ORDER[i : i + per_word])) for i in range(0, len(ORDER), per_word)]
+
+    @pl.loop(0, len(ORDER))
     def _(step):
-        gathering = step < 4
-        computing = jnp.logical_and(step >= 1, step < 5)
-        sending = jnp.logical_and(step >= 2, step < 5)
-        reducing = step >= 3
-        at_c, at_r = step - 1, step - 2
-
-        @pl.when(step == 2)
-        def _():
-            shift(3)
-
-        @pl.when(gathering)
-        def _():
-            gather_a(step)
-
-        @pl.when(reducing)
-        def _():
-            reduce_2(at_r % 3)
-
-        @pl.when(step == 4)
-        def _():
-            reduce_1a(0)
-            reduce_1b(0)
-
-        @pl.when(step >= 4)
-        def _():
-            reduce_5(step - 3)
-
-        @pl.when(computing)
-        def _():
-            gather_e(at_c)
-
-        @pl.when(step == 0)
-        def _():
-            gather_e(RAW)
-            fill_slots()
-            for part in range(3):
-                shift(part)
-
-        @pl.when(step == 1)
-        def _():
-            for load in loads:
-                load.wait()
-
-        @pl.when(computing)
-        def _():
-            complete(at_c)
-            project(at_c, 0, 2)
-
-        @pl.when(gathering)
-        def _():
-            gather_b(step)
-
-        @pl.when(computing)
-        def _():
-            project(at_c, 2, 4)
-
-        @pl.when(gathering)
-        def _():
-            gather_c(step)
-
-        @pl.when(step < 2)
-        def _():
-            gather_own(step + 2)
-
-        @pl.when(computing)
-        def _():
-            activate()
-            gather_sent(at_c)
-            lower_rows(at_c, 0, 2)
-
-        @pl.when(sending)
-        def _():
-            reduce_1a(at_c)
-
-        @pl.when(gathering)
-        def _():
-            gather_d(step)
-
-        @pl.when(computing)
-        def _():
-            lower_rows(at_c, 2, 4)
-
-        @pl.when(sending)
-        def _():
-            reduce_1b(at_c)
-
-        @pl.when(reducing)
-        def _():
-            reduce_3(at_r, (0,))
-
-        @pl.when(step == 4)
-        def _():
-            reduce_2(3)
-
-        @pl.when(reducing)
-        def _():
-            reduce_3(at_r, (1, 2, 3))
-
-        @pl.when(step == 5)
-        def _():
-            reduce_3(0, (0,))
-
-    reduce_3(0, (1, 2, 3))
-    reduce_5(3)
-    reduce_5(0)
+        at = step // per_word
+        word = jnp.int32(words[0])
+        for i in range(1, len(words)):
+            word = jnp.where(at == i, jnp.int32(words[i]), word)
+        code = lax.shift_right_logical(word, 7 * (step % per_word)) % 128
+        take(code // 4, code % 4, 0, len(steps))
+
     gather_sent(RAW)
     shift_copy(0, 1 - core).wait_send()
     in_copy(0, 1 - core).wait_send()
@@ -547,7 +513,6 @@
             vmem((units, width), BF16),
             vmem((units, width), BF16),
             vmem((8, 16, split // 2), BF16),
-            vmem((4, 2, 16, split // 2), BF16),
             vmem((4, 2, 16, half), BF16),
             vmem((8, 16, half), BF16),
             vmem((4, 4, 4, 16, width), BF16),

time: 168 us -> 162 us (0.964)
  Pallas kernels: 166 us -> 160 us
    pallas_call x1, Pallas kernels: 166 us -> 160 us  [per_device(): pl.pallas_call(ffn_kernel, out_shape=jax.ShapeDtypeStruct((row_count, wid...]
where the time goes in v5:
time: 162 us
  Pallas kernels  160 us (99%)
  local copies, waits for them, and re-layouts  1.82 us (1%)
    pallas_call x1, Pallas kernels, per_device(): pl.pallas_call(ffn_kernel, out_shape=jax.ShapeDtypeStruct((row_count, wid...  160 us

profile of v5, /device:TPU:1, one launch (start us, length us, event | category | flops | bytes accessed | tf_op | source)
XLA Modules:
  0.0 161.8 jit_solution(8341241529338175783)
XLA Ops:
  0.0 160.0 %shard_map.64 = bf16[32,7168]{1,0:T(8,128)(2,1)} custom-call(bf16[32,7168]{1,0:T(8,128)(2,1)} %hidden.1, s32[1,32]{1,0:T(1,128)} %bitcast.7, f32[1,7168]{1,0:T(1,128)} %bitcast.6, bf16[1,576,7168]{2,1,0:T(8,128)(2,1)} %bitcast.4, bf16[1,576,7168]{2,1,0:T(8,128)(2,1)} %bitcast.5, bf16[1,576,7168]{2,1,0:T(8,128)(2,1)} %down_hbm.1), custom_call_target="tpu_custom_call" | custom-call | tf_op jit(solution)/shard_map/pallas_call | solution.py:506
  160.0 1.8 %copy.8 = bf16[32,7168]{1,0:T(8,128)(2,1)} copy(bf16[32,7168]{1,0:T(8,128)(2,1)} %shard_map.64) | data formatting | bytes 917504

commit v6 on v5

--- a/solution.py
+++ b/solution.py
@@ -17,11 +17,12 @@
 RAW = 4
 
 ORDER = (
-    4, 88, 8, 12, 1, 92, 2, 16, 96, 20, 5, 9, 24, 13, 17, 3, 28, 21, 6, 32,
-    36, 40, 10, 14, 7, 100, 25, 29, 18, 22, 33, 11, 37, 45, 41, 49, 53, 15, 19, 26,
-    23, 57, 61, 30, 65, 69, 34, 38, 46, 42, 50, 27, 54, 73, 77, 58, 31, 62, 66, 44,
-    35, 70, 39, 47, 81, 48, 43, 51, 85, 55, 59, 63, 74, 67, 71, 78, 52, 56, 60, 64,
-    68, 75, 82, 86, 79, 72, 76, 83, 80, 87, 84,
+    4, 88, 8, 1, 92, 12, 16, 96, 20, 5, 9, 2, 24, 28, 13, 17, 32, 21, 6, 36,
+    10, 25, 100, 3, 40, 14, 29, 18, 33, 22, 7, 37, 41, 45, 49, 11, 26, 30, 53, 57,
+    34, 15, 38, 19, 61, 23, 65, 42, 46, 50, 69, 27, 31, 54, 58, 62, 66, 44, 35, 48,
+    39, 43, 70, 73, 77, 47, 51, 74, 78, 81, 85, 55, 59, 63, 67, 82, 71, 86, 52, 56,
+    75, 79, 60, 64, 83, 104, 108, 112, 68, 116, 120, 124, 128, 87, 132, 72, 76, 80, 136, 140,
+    144, 84, 148,
 )
 
 
@@ -46,7 +47,7 @@
     w_gate, w_up, w_down, blocks_out, blocks_back, returned, rows, raw, slots,
     gate_sum, up_sum, mid,
     near_y1, near_z1, near_y2, near_z2, far_z1, far_y1, far_z2, far_y2,
-    w_sem, in_send, in_recv, shift_send, shift_recv, home_sem, back_send, back_recv, gather_send, gather_recv, reduce_send, reduce_recv,
+    w_sem, in_send, in_recv, shift_send, shift_recv, home_sem, column_send, column_recv, free_sem, back_send, back_recv, gather_send, gather_recv, reduce_send, reduce_recv,
 ):
     att, ffn = lax.axis_index("att"), lax.axis_index("ffn")
     x, core = att // 2, att % 2
@@ -54,13 +55,11 @@
     yp, y2, ym = (y + 1) % 4, (y + 2) % 4, (y + 3) % 4
     zp, z2, zm = (z + 1) % 4, (z + 2) % 4, (z + 3) % 4
     width = hidden.shape[1]
-    half, quarter = width // 2, width // 4
-    a_cols, b_cols = pl.ds(0, half), pl.ds(half, half)
-    q = [pl.ds(i * quarter, quarter) for i in range(4)]
+    quarter = width // 4
     extra = raw_columns(width)
     split = width - extra
     g_half, x_half = split // 2, extra // 2
-    slot_geometry, raw_geometry = halves(split), halves(2 * extra + 256)
+    slot_geometry, raw_geometry, sum_geometry = halves(split), halves(2 * extra + 256), halves(2 * extra)
     z_plus, z_minus, y_plus, y_minus = (att, y * 4 + zp), (att, y * 4 + zm), (att, yp * 4 + z), (att, ym * 4 + z)
     ALL = pl.ds(0, 4)
 
@@ -208,10 +207,6 @@
             for link in range(4):
                 g_wait(part, link, event, g[(link + 2) % 4])
 
-    def wait_units(sem, part, units):
-        piece = rows.at[part, 0, pl.ds(0, units)] if units <= 4 else rows.at[part, pl.ds(0, units // 4)]
-        pltpu.make_async_copy(piece, piece, sem).wait()
-
     def gather_sent(part):
         for event, units in enumerate((4, 1, 2, 2, 2, 1, 1, 1, 1)):
             if part is RAW:
@@ -220,15 +215,18 @@
                 piece = rows.at[part, 0, pl.ds(0, units), :, slot_geometry[0]]
             pltpu.make_async_copy(piece, piece, gather_send.at[part, event]).wait()
 
+    def slot_table(of_y, of_z, lane):
+        where = jnp.concatenate([raw[of_y, of_z, :, pl.ds(2 * extra + 128 * j, 128)] for j in (0, 1)], axis=0)
+        where = where.astype(F32).astype(jnp.int32)
+        return jnp.concatenate([(lane == where).astype(F32), (lane == where + 8).astype(F32)], axis=0).astype(BF16)
+
     def fill_slots():
         lane = lax.broadcasted_iota(jnp.int32, (32, 128), 1)
 
         @pl.loop(0, 16)
         def _(i):
             of_y, of_z = i // 4, i % 4
-            where = jnp.concatenate([raw[of_y, of_z, :, pl.ds(2 * extra + 128 * j, 128)] for j in (0, 1)], axis=0)
-            where = where.astype(F32).astype(jnp.int32)
-            table = jnp.concatenate([(lane == where).astype(F32), (lane == where + 8).astype(F32)], axis=0).astype(BF16)
+            table = slot_table(of_y, of_z, lane)
             lines = [raw[of_y, of_z, :, pl.ds(extra * j + x_half * k, x_half)] for k in (0, 1) for j in (0, 1)]
             filled = lax.dot_general(table, jnp.concatenate(lines, axis=0), FIRST, preferred_element_type=F32)
             slots[:, of_y, of_z] = filled.astype(BF16).reshape(8, 16, x_half)
@@ -270,6 +268,9 @@
             wait_shift(part, 0)
             wait_shift(part, 1)
 
+        complete_again(part)
+
+    def complete_again(part):
         @pl.loop(0, 16)
         def _(i):
             of_y, of_z = i // 4, i % 4
@@ -306,10 +307,19 @@
 
     def lower_rows(part, lower):
         @pl.loop(lower, lower + 2)
-        def _(i):
-            cols = pl.ds(pl.multiple_of(i * quarter, quarter), quarter)
+        def _(step):
+            cols = pl.ds(pl.multiple_of((3 - step) * quarter, quarter), quarter)
             partial = jnp.dot(mid[...], w_down[:, cols], preferred_element_type=F32)
             rows[part, :, :, :, cols] = partial.astype(BF16).reshape(4, 4, 16, quarter)
+
+    def sums(part):
+        return sum_geometry if part is RAW else slot_geometry
+
+    def landing(part):
+        return 1 if part is RAW else part * 2 // 3
+
+    def place_at(buffer, part, cols, *index):
+        return buffer.at[(landing(part), *index, slice(None), pl.ds(0, cols.size))]
 
     def r_send(part, link, event, src, dst):
         pltpu.make_async_remote_copy(
@@ -321,60 +331,70 @@
     def r_wait(part, link, event, dst):
         pltpu.make_async_copy(dst, dst, reduce_recv.at[part, link, event]).wait()
 
-    def add(index, *terms):
-        total = rows[index].astype(F32)
+    def add(piece, *terms):
+        total = piece[...].astype(F32)
         for term in terms:
-            total = total + term.astype(F32)
-        rows[index] = total.astype(BF16)
+            total = total + term[...].astype(F32)
+        piece[...] = total.astype(BF16)
 
     across_z, across_y = (z2, zp, zm, z), (y2, yp, ym, y)
 
-    def landing(part):
-        return part * 2 // 3
-
     def reduce_1a(part):
+        q = sums(part)[3]
         for i in range(4):
-            r_send(part, 2, i, rows.at[part, y2, across_z[i], :, q[0]], near_y1.at[landing(part), 0, i])
-            r_send(part, 3, i, rows.at[part, y2, across_z[i], :, q[1]], near_y1.at[landing(part), 1, i])
+            for side in range(2):
+                cols = q[side]
+                r_send(part, 2 + side, i, unit(part, y2, across_z[i], cols), place_at(near_y1, part, cols, side, i))
 
     def reduce_1b(part):
+        q = sums(part)[3]
         for i in range(4):
-            r_send(part, 0, i, rows.at[part, across_y[i], z2, :, q[2]], near_z1.at[landing(part), 0, i])
-            r_send(part, 1, i, rows.at[part, across_y[i], z2, :, q[3]], near_z1.at[landing(part), 1, i])
+            for side in range(2):
+                cols = q[2 + side]
+                r_send(part, side, i, unit(part, across_y[i], z2, cols), place_at(near_z1, part, cols, side, i))
 
     def reduce_2(part, pieces):
+        _, a_cols, b_cols, q = sums(part)
         for i in pieces:
             at_y, at_z = across_y[i], across_z[i]
             for side, goal in ((0, yp), (1, ym)):
-                r_wait(part, 2 + side, i, near_y1.at[landing(part), side, i])
-                add((part, goal, at_z, slice(None), q[side]), near_y1[landing(part), side, i])
-                r_send(part, 2 + side, 4 + i, rows.at[part, goal, at_z, :, a_cols], near_y2.at[landing(part), side, i])
+                landed = place_at(near_y1, part, q[side], side, i)
+                r_wait(part, 2 + side, i, landed)
+                add(unit(part, goal, at_z, q[side]), landed)
+                r_send(part, 2 + side, 4 + i, unit(part, goal, at_z, a_cols), place_at(near_y2, part, a_cols, side, i))
             for side, goal in ((0, zp), (1, zm)):
-                r_wait(part, side, i, near_z1.at[landing(part), side, i])
-                add((part, at_y, goal, slice(None), q[2 + side]), near_z1[landing(part), side, i])
-                r_send(part, side, 4 + i, rows.at[part, at_y, goal, :, b_cols], near_z2.at[landing(part), side, i])
+                landed = place_at(near_z1, part, q[2 + side], side, i)
+                r_wait(part, side, i, landed)
+                add(unit(part, at_y, goal, q[2 + side]), landed)
+                r_send(part, side, 4 + i, unit(part, at_y, goal, b_cols), place_at(near_z2, part, b_cols, side, i))
 
     def reduce_3(part, pieces):
+        _, a_cols, b_cols, q = sums(part)
         for i in pieces:
             at_y, at_z = across_y[i], across_z[i]
-            r_wait(part, 2, 4 + i, near_y2.at[landing(part), 0, i])
-            r_wait(part, 3, 4 + i, near_y2.at[landing(part), 1, i])
-            add((part, y, at_z, slice(None), a_cols), near_y2[landing(part), 0, i], near_y2[landing(part), 1, i])
-            r_wait(part, 0, 4 + i, near_z2.at[landing(part), 0, i])
-            r_wait(part, 1, 4 + i, near_z2.at[landing(part), 1, i])
-            add((part, at_y, z, slice(None), b_cols), near_z2[landing(part), 0, i], near_z2[landing(part), 1, i])
+            landed = [place_at(near_y2, part, a_cols, side, i) for side in range(2)]
+            r_wait(part, 2, 4 + i, landed[0])
+            r_wait(part, 3, 4 + i, landed[1])
+            add(unit(part, y, at_z, a_cols), *landed)
+            landed = [place_at(near_z2, part, b_cols, side, i) for side in range(2)]
+            r_wait(part, 0, 4 + i, landed[0])
+            r_wait(part, 1, 4 + i, landed[1])
+            add(unit(part, at_y, z, b_cols), *landed)
             if i == 0:
                 for side in range(2):
-                    r_send(part, side, 8, rows.at[part, y, z2, :, q[side]], far_z1.at[landing(part), side])
-                    r_send(part, 2 + side, 8, rows.at[part, y2, z, :, q[2 + side]], far_y1.at[landing(part), side])
+                    r_send(part, side, 8, unit(part, y, z2, q[side]), place_at(far_z1, part, q[side], side))
+                    cols = q[2 + side]
+                    r_send(part, 2 + side, 8, unit(part, y2, z, cols), place_at(far_y1, part, cols, side))
             elif i < 3:
                 side = i - 1
-                r_wait(part, side, 8, far_z1.at[landing(part), side])
-                add((part, y, at_z, slice(None), q[side]), far_z1[landing(part), side])
-                r_send(part, side, 9, rows.at[part, y, at_z, :, a_cols], far_z2.at[landing(part), side])
-                r_wait(part, 2 + side, 8, far_y1.at[landing(part), side])
-                add((part, at_y, z, slice(None), q[2 + side]), far_y1[landing(part), side])
-                r_send(part, 2 + side, 9, rows.at[part, at_y, z, :, b_cols], far_y2.at[landing(part), side])
+                landed = place_at(far_z1, part, q[side], side)
+                r_wait(part, side, 8, landed)
+                add(unit(part, y, at_z, q[side]), landed)
+                r_send(part, side, 9, unit(part, y, at_z, a_cols), place_at(far_z2, part, a_cols, side))
+                landed = place_at(far_y1, part, q[2 + side], side)
+                r_wait(part, 2 + side, 8, landed)
+                add(unit(part, at_y, z, q[2 + side]), landed)
+                r_send(part, 2 + side, 9, unit(part, at_y, z, b_cols), place_at(far_y2, part, b_cols, side))
 
     def back_copy(part, to_core):
         dest = ((x + chip_offset(part)) % 4) * 2 + to_core
@@ -385,27 +405,106 @@
         )
 
     def reduce_5(part):
+        whole, a_cols, b_cols, _ = sums(part)
+        left, right = unit(part, y, z, a_cols)[...].astype(F32), unit(part, y, z, b_cols)[...].astype(F32)
         for side in range(2):
-            r_wait(part, side, 9, far_z2.at[landing(part), side])
-            r_wait(part, 2 + side, 9, far_y2.at[landing(part), side])
-        left = rows[part, y, z, :, a_cols].astype(F32) + far_z2[landing(part), 0].astype(F32) + far_z2[landing(part), 1].astype(F32)
-        right = rows[part, y, z, :, b_cols].astype(F32) + far_y2[landing(part), 0].astype(F32) + far_y2[landing(part), 1].astype(F32)
-        for to_core in range(2):
-            lines = slice(8 * to_core, 8 * to_core + 8)
-            blocks_back[part, to_core] = jnp.concatenate([left[lines], right[lines]], axis=0).astype(BF16)
+            landed = place_at(far_z2, part, a_cols, side)
+            r_wait(part, side, 9, landed)
+            left = left + landed[...].astype(F32)
+            landed = place_at(far_y2, part, b_cols, side)
+            r_wait(part, 2 + side, 9, landed)
+            right = right + landed[...].astype(F32)
+        if part is RAW:
+            out[:16, split:] = (hidden[:16, split:].astype(F32) + left.astype(BF16).astype(F32)).astype(BF16)
+            out[16:, split:] = (hidden[16:, split:].astype(F32) + right.astype(BF16).astype(F32)).astype(BF16)
+        else:
+            for to_core in range(2):
+                lines = slice(8 * to_core, 8 * to_core + 8)
+                blocks_back[part, to_core] = jnp.concatenate([left[lines], right[lines]], axis=0).astype(BF16)
+
+            @pl.when(part == 0)
+            def _():
+                back_copy(part, 1 - core).start()
+                returned[att] = blocks_back[part, core]
+
+            @pl.when(part > 0)
+            def _():
+                back_copy(part, 0).start()
+                back_copy(part, 1).start()
+
+        for event, units in enumerate((4, 8, 1, 2)):
+            many = (0, pl.ds(0, units)) if units <= 4 else (pl.ds(0, units // 4),)
+            if part is RAW:
+                piece = raw_units(many, whole)
+            else:
+                piece = part_units(part, many, whole)
+            pltpu.make_async_copy(piece, piece, reduce_send.at[part, event]).wait()
+
+    def raw_units(many, cols):
+        return raw.at[many[0], many[1], :, cols] if len(many) == 2 else raw.at[many[0], :, :, cols]
+
+    def part_units(part, many, cols):
+        return rows.at[part, many[0], many[1], :, cols] if len(many) == 2 else rows.at[part, many[0], :, :, cols]
+
+    def column_copy(part, to_core):
+        dest = ((x + chip_offset(part)) % 4) * 2 + to_core
+        return pltpu.make_async_remote_copy(
+            src_ref=shifted(part, to_core), dst_ref=slots.at[att],
+            send_sem=column_send.at[part, to_core], recv_sem=column_recv.at[att],
+            device_id=(dest, ffn), device_id_type=MESH,
+        )
+
+    def column_home():
+        return pltpu.make_async_copy(shifted(0, core), slots.at[att], home_sem)
+
+    def free_slots(part):
+        def free(to_core):
+            dest = ((x + 4 - chip_offset(part)) % 4) * 2 + to_core
+            shift_copy(part, to_core).wait_send()
+            pl.semaphore_signal(free_sem.at[att], inc=1, device_id=(dest, ffn), device_id_type=MESH)
 
         @pl.when(part == 0)
         def _():
-            back_copy(part, 1 - core).start()
-            returned[att] = blocks_back[part, core]
+            free(1 - core)
 
         @pl.when(part > 0)
         def _():
-            back_copy(part, 0).start()
-            back_copy(part, 1).start()
-
-        for event, units in enumerate((4, 8, 1, 2)):
-            wait_units(reduce_send.at[part, event], part, units)
+            free(0)
+            free(1)
+
+    def return_columns(part):
+        complete_again(part)
+
+        @pl.when(part == 0)
+        def _():
+            column_home().start()
+            pl.semaphore_wait(free_sem.at[x * 2 + 1 - core], 1)
+            column_copy(0, 1 - core).start()
+
+        @pl.when(part > 0)
+        def _():
+            for to_core in range(2):
+                pl.semaphore_wait(free_sem.at[((x + chip_offset(part)) % 4) * 2 + to_core], 1)
+                column_copy(part, to_core).start()
+
+    def collect():
+        column_home().wait()
+        for step in range(1, 8):
+            source = (att + step) % 8
+            pltpu.make_async_copy(slots.at[0], slots.at[source], column_recv.at[source]).wait()
+        gather_sent(RAW)
+        lane = lax.broadcasted_iota(jnp.int32, (32, 128), 1)
+
+        @pl.loop(0, 16)
+        def _(i):
+            of_y, of_z = i // 4, i % 4
+            table = slot_table(of_y, of_z, lane)
+            lines = slots[:, of_y, of_z].reshape(128, x_half)
+            sums_of = jnp.dot(table, lines, preferred_element_type=F32).astype(BF16)
+            for j in range(2):
+                for k in range(2):
+                    start = 32 * k + 16 * j
+                    raw[of_y, of_z, :, pl.ds(extra * j + x_half * k, x_half)] = sums_of[start : start + 16]
 
     send_own(RAW)
     in_copy(0, 1 - core).start()
@@ -423,6 +522,7 @@
         @pl.when(jnp.logical_not(second))
         def _():
             complete(part)
+            free_slots(part)
 
         project(part, jnp.where(second, 2, 0))
 
@@ -433,6 +533,10 @@
             gather_sent(part)
 
         lower_rows(part, jnp.where(second, 2, 0))
+
+        @pl.when(jnp.logical_not(second))
+        def _():
+            return_columns(part)
 
     def spread(part):
         for load in loads:
@@ -448,6 +552,10 @@
         *[functools.partial(reduce_3, pieces=(i,)) for i in range(4)],
         reduce_5,
         lambda part: gather_f(RAW), lambda part: gather_e(RAW), spread, lambda part: shift(3),
+        lambda part: collect(), lambda part: reduce_1a(RAW), lambda part: reduce_1b(RAW),
+        *[lambda part, i=i: reduce_2(RAW, (i,)) for i in range(4)],
+        *[lambda part, i=i: reduce_3(RAW, (i,)) for i in range(4)],
+        lambda part: reduce_5(RAW),
     ]
 
     def take(kind, part, low, high):
@@ -463,8 +571,8 @@
                 kind < middle, lambda: take(kind, part, low, middle), lambda: take(kind, part, middle, high)
             )
 
-    per_word = 4
-    words = [sum(code << (7 * k) for k, code in enumerate(ORDER[i : i + per_word])) for i in range(0, len(ORDER), per_word)]
+    per_word = 3
+    words = [sum(code << (8 * k) for k, code in enumerate(ORDER[i : i + per_word])) for i in range(0, len(ORDER), per_word)]
 
     @pl.loop(0, len(ORDER))
     def _(step):
@@ -472,36 +580,32 @@
         word = jnp.int32(words[0])
         for i in range(1, len(words)):
             word = jnp.where(at == i, jnp.int32(words[i]), word)
-        code = lax.shift_right_logical(word, 7 * (step % per_word)) % 128
+        code = lax.shift_right_logical(word, 8 * (step % per_word)) % 256
         take(code // 4, code % 4, 0, len(steps))
 
-    gather_sent(RAW)
-    shift_copy(0, 1 - core).wait_send()
+    column_copy(0, 1 - core).wait_send()
     in_copy(0, 1 - core).wait_send()
     back_copy(0, 1 - core).wait_send()
     for part in range(1, 4):
         for to_core in range(2):
-            shift_copy(part, to_core).wait_send()
+            column_copy(part, to_core).wait_send()
             in_copy(part, to_core).wait_send()
             back_copy(part, to_core).wait_send()
     for step in range(1, 8):
         source = (att + step) % 8
         pltpu.make_async_copy(blocks_back.at[0, 0], returned.at[source], back_recv.at[source]).wait()
-    lines = returned[...].reshape(128, half)
-    out[:, :half] = (
-        hidden[:, :half].astype(F32) + lax.dot_general(table_a, lines, FIRST, preferred_element_type=F32)
-    ).astype(BF16)
-    out[:, half:] = (
-        hidden[:, half:].astype(F32) + lax.dot_general(table_b, lines, FIRST, preferred_element_type=F32)
-    ).astype(BF16)
+    lines = returned[...].reshape(128, g_half)
+    for table, cols in ((table_a, slice(0, g_half)), (table_b, slice(g_half, split))):
+        found = lax.dot_general(table, lines, FIRST, preferred_element_type=F32)
+        out[:, cols] = (hidden[:, cols].astype(F32) + found).astype(BF16)
 
 
 def per_device(hidden, route, norm_gain, gate_weight, up_weight, down_weight):
     row_count, width = hidden.shape
     units = gate_weight.shape[2]
-    half, quarter = width // 2, width // 4
     extra = raw_columns(width)
     split = width - extra
+    more = halves(split)[3][0].size
     vmem, dma = pltpu.VMEM, pltpu.SemaphoreType.DMA
     return pl.pallas_call(
         ffn_kernel,
@@ -513,22 +617,22 @@
             vmem((units, width), BF16),
             vmem((units, width), BF16),
             vmem((8, 16, split // 2), BF16),
-            vmem((4, 2, 16, half), BF16),
-            vmem((8, 16, half), BF16),
+            vmem((4, 2, 16, split // 2), BF16),
+            vmem((8, 16, split // 2), BF16),
             vmem((4, 4, 4, 16, width), BF16),
             vmem((4, 4, 16, 2 * extra + 256), BF16),
             vmem((8, 4, 4, 16, extra // 2), BF16),
             vmem((units, 256), F32),
             vmem((units, 256), F32),
             vmem((256, units), BF16),
-            vmem((3, 2, 4, 16, quarter), BF16),
-            vmem((3, 2, 4, 16, quarter), BF16),
-            vmem((3, 2, 4, 16, half), BF16),
-            vmem((3, 2, 4, 16, half), BF16),
-            vmem((3, 2, 16, quarter), BF16),
-            vmem((3, 2, 16, quarter), BF16),
-            vmem((3, 2, 16, half), BF16),
-            vmem((3, 2, 16, half), BF16),
+            vmem((3, 2, 4, 16, more), BF16),
+            vmem((3, 2, 4, 16, more), BF16),
+            vmem((3, 2, 4, 16, split // 2), BF16),
+            vmem((3, 2, 4, 16, split // 2), BF16),
+            vmem((3, 2, 16, more), BF16),
+            vmem((3, 2, 16, more), BF16),
+            vmem((3, 2, 16, split // 2), BF16),
+            vmem((3, 2, 16, split // 2), BF16),
             dma((3,)),
             dma((4, 2)),
             dma((4, 2)),
@@ -537,10 +641,13 @@
             dma,
             dma((4, 2)),
             dma((8,)),
+            pltpu.SemaphoreType.REGULAR((8,)),
+            dma((4, 2)),
+            dma((8,)),
             dma((5, 9)),
             dma((5, 4, 9)),
-            dma((4, 4)),
-            dma((4, 4, 10)),
+            dma((5, 4)),
+            dma((5, 4, 10)),
         ],
         compiler_params=pltpu.CompilerParams(
             collective_id=0, has_side_effects=True, vmem_limit_bytes=63 * 1024 * 1024

time: 162 us -> 151 us (0.932)
  Pallas kernels: 160 us -> 149 us
    pallas_call x1, Pallas kernels: 160 us -> 149 us  [per_device(): pl.pallas_call(ffn_kernel, out_shape=jax.ShapeDtypeStruct((row_count, wid...]
where the time goes in v6:
time: 151 us
  Pallas kernels  149 us (99%)
  local copies, waits for them, and re-layouts  1.82 us (1%)
    pallas_call x1, Pallas kernels, per_device(): pl.pallas_call(ffn_kernel, out_shape=jax.ShapeDtypeStruct((row_count, wid...  149 us

profile of v6, /device:TPU:1, one launch (start us, length us, event | category | flops | bytes accessed | tf_op | source)
XLA Modules:
  0.0 151.2 jit_solution(4367028055114488158)
XLA Ops:
  0.0 149.4 %shard_map.64 = bf16[32,7168]{1,0:T(8,128)(2,1)} custom-call(bf16[32,7168]{1,0:T(8,128)(2,1)} %hidden.1, s32[1,32]{1,0:T(1,128)} %bitcast.7, f32[1,7168]{1,0:T(1,128)} %bitcast.6, bf16[1,576,7168]{2,1,0:T(8,128)(2,1)} %bitcast.4, bf16[1,576,7168]{2,1,0:T(8,128)(2,1)} %bitcast.5, bf16[1,576,7168]{2,1,0:T(8,128)(2,1)} %down_hbm.1), custom_call_target="tpu_custom_call" | custom-call | tf_op jit(solution)/shard_map/pallas_call | solution.py:610
  149.4 1.8 %copy.8 = bf16[32,7168]{1,0:T(8,128)(2,1)} copy(bf16[32,7168]{1,0:T(8,128)(2,1)} %shard_map.64) | data formatting | bytes 917504

commit v7 on v6

--- a/solution.py
+++ b/solution.py
@@ -22,7 +22,7 @@
     34, 15, 38, 19, 61, 23, 65, 42, 46, 50, 69, 27, 31, 54, 58, 62, 66, 44, 35, 48,
     39, 43, 70, 73, 77, 47, 51, 74, 78, 81, 85, 55, 59, 63, 67, 82, 71, 86, 52, 56,
     75, 79, 60, 64, 83, 104, 108, 112, 68, 116, 120, 124, 128, 87, 132, 72, 76, 80, 136, 140,
-    144, 84, 148,
+    144, 84,
 )
 
 
@@ -43,8 +43,8 @@
 
 
 def ffn_kernel(
-    hidden, route, gain, gate_hbm, up_hbm, down_hbm, out,
-    w_gate, w_up, w_down, blocks_out, blocks_back, returned, rows, raw, slots,
+    hidden_hbm, route, gain, gate_hbm, up_hbm, down_hbm, out,
+    w_gate, w_up, w_down, blocks_out, blocks_back, returned, rows, raw, slots, hidden,
     gate_sum, up_sum, mid,
     near_y1, near_z1, near_y2, near_z2, far_z1, far_y1, far_z2, far_y2,
     w_sem, in_send, in_recv, shift_send, shift_recv, home_sem, column_send, column_recv, free_sem, back_send, back_recv, gather_send, gather_recv, reduce_send, reduce_recv,
@@ -54,7 +54,7 @@
     y, z = ffn // 4, ffn % 4
     yp, y2, ym = (y + 1) % 4, (y + 2) % 4, (y + 3) % 4
     zp, z2, zm = (z + 1) % 4, (z + 2) % 4, (z + 3) % 4
-    width = hidden.shape[1]
+    width = hidden_hbm.shape[1]
     quarter = width // 4
     extra = raw_columns(width)
     split = width - extra
@@ -63,6 +63,8 @@
     z_plus, z_minus, y_plus, y_minus = (att, y * 4 + zp), (att, y * 4 + zm), (att, yp * 4 + z), (att, ym * 4 + z)
     ALL = pl.ds(0, 4)
 
+    fetch = pltpu.make_async_copy(hidden_hbm, hidden, home_sem)
+    fetch.start()
     barrier = pltpu.get_barrier_semaphore()
     for other in (z_plus, z_minus, y_plus, y_minus):
         pl.semaphore_signal(barrier, inc=1, device_id=other, device_id_type=MESH)
@@ -75,6 +77,7 @@
     for load in loads:
         load.start()
 
+    fetch.wait()
     widened = hidden[...].astype(F32)
     scale = lax.rsqrt(jnp.mean(widened * widened, axis=-1, keepdims=True) + 1e-06)
     normed = (widened * scale * gain[...]).astype(BF16)
@@ -555,7 +558,6 @@
         lambda part: collect(), lambda part: reduce_1a(RAW), lambda part: reduce_1b(RAW),
         *[lambda part, i=i: reduce_2(RAW, (i,)) for i in range(4)],
         *[lambda part, i=i: reduce_3(RAW, (i,)) for i in range(4)],
-        lambda part: reduce_5(RAW),
     ]
 
     def take(kind, part, low, high):
@@ -598,6 +600,7 @@
     for table, cols in ((table_a, slice(0, g_half)), (table_b, slice(g_half, split))):
         found = lax.dot_general(table, lines, FIRST, preferred_element_type=F32)
         out[:, cols] = (hidden[:, cols].astype(F32) + found).astype(BF16)
+    reduce_5(RAW)
 
 
 def per_device(hidden, route, norm_gain, gate_weight, up_weight, down_weight):
@@ -610,7 +613,7 @@
     return pl.pallas_call(
         ffn_kernel,
         out_shape=jax.ShapeDtypeStruct((row_count, width), BF16),
-        in_specs=[pl.BlockSpec(memory_space=vmem)] * 3 + [pl.BlockSpec(memory_space=pl.ANY)] * 3,
+        in_specs=[pl.BlockSpec(memory_space=pl.ANY)] + [pl.BlockSpec(memory_space=vmem)] * 2 + [pl.BlockSpec(memory_space=pl.ANY)] * 3,
         out_specs=pl.BlockSpec(memory_space=vmem),
         scratch_shapes=[
             vmem((units, width), BF16),
@@ -622,6 +625,7 @@
             vmem((4, 4, 4, 16, width), BF16),
             vmem((4, 4, 16, 2 * extra + 256), BF16),
             vmem((8, 4, 4, 16, extra // 2), BF16),
+            vmem((row_count, width), BF16),
             vmem((units, 256), F32),
             vmem((units, 256), F32),
             vmem((256, units), BF16),

time: 151 us -> 151 us (level)
  no operation moved by 1% of the time
where the time goes in v7:
time: 151 us; the launch traced here: 150 us
  Pallas kernels  149 us (99%)
  local copies, waits for them, and re-layouts  1.82 us (1%)
    pallas_call x1, Pallas kernels, per_device(): pl.pallas_call(ffn_kernel, out_shape=jax.ShapeDtypeStruct((row_count, wid...  149 us

profile of v7, /device:TPU:1, one launch (start us, length us, event | category | flops | bytes accessed | tf_op | source)
XLA Modules:
  0.0 150.4 jit_solution(11084587913652829833)
XLA Ops:
  0.0 148.5 %shard_map.64 = bf16[32,7168]{1,0:T(8,128)(2,1)} custom-call(bf16[32,7168]{1,0:T(8,128)(2,1)} %hidden_hbm.1, s32[1,32]{1,0:T(1,128)} %bitcast.7, f32[1,7168]{1,0:T(1,128)} %bitcast.6, bf16[1,576,7168]{2,1,0:T(8,128)(2,1)} %bitcast.4, bf16[1,576,7168]{2,1,0:T(8,128)(2,1)} %bitcast.5, bf16[1,576,7168]{2,1,0:T(8,128)(2,1)} %down_hbm.1), custom_call_target="tpu_custom_call" | custom-call | tf_op jit(solution)/shard_map/pallas_call | solution.py:613
  148.5 1.8 %copy.8 = bf16[32,7168]{1,0:T(8,128)(2,1)} copy(bf16[32,7168]{1,0:T(8,128)(2,1)} %shard_map.64) | data formatting | bytes 917504

commit v8 on v7

--- a/solution.py
+++ b/solution.py
@@ -573,16 +573,19 @@
                 kind < middle, lambda: take(kind, part, low, middle), lambda: take(kind, part, middle, high)
             )
 
-    per_word = 3
+    per_word = 4
     words = [sum(code << (8 * k) for k, code in enumerate(ORDER[i : i + per_word])) for i in range(0, len(ORDER), per_word)]
+    words = [word - (1 << 32) if word >= 1 << 31 else word for word in words]
 
     @pl.loop(0, len(ORDER))
     def _(step):
         at = step // per_word
-        word = jnp.int32(words[0])
-        for i in range(1, len(words)):
-            word = jnp.where(at == i, jnp.int32(words[i]), word)
-        code = lax.shift_right_logical(word, 8 * (step % per_word)) % 256
+        left = [jnp.int32(word) for word in words]
+        while len(left) > 1:
+            odd = at % 2 == 1
+            left = [jnp.where(odd, *left[i : i + 2][::-1]) if i + 1 < len(left) else left[i] for i in range(0, len(left), 2)]
+            at = at // 2
+        code = lax.shift_right_logical(left[0], 8 * (step % per_word)) % 256
         take(code // 4, code % 4, 0, len(steps))
 
     column_copy(0, 1 - core).wait_send()

time: 151 us -> 151 us (level)
  no operation moved by 1% of the time
where the time goes in v8:
time: 151 us; the launch traced here: 150 us
  Pallas kernels  149 us (99%)
  local copies, waits for them, and re-layouts  1.82 us (1%)
    pallas_call x1, Pallas kernels, per_device(): pl.pallas_call(ffn_kernel, out_shape=jax.ShapeDtypeStruct((row_count, wid...  149 us

profile of v8, /device:TPU:1, one launch (start us, length us, event | category | flops | bytes accessed | tf_op | source)
XLA Modules:
  0.0 150.4 jit_solution(13822300218538152188)
XLA Ops:
  0.0 148.5 %shard_map.64 = bf16[32,7168]{1,0:T(8,128)(2,1)} custom-call(bf16[32,7168]{1,0:T(8,128)(2,1)} %hidden_hbm.1, s32[1,32]{1,0:T(1,128)} %bitcast.7, f32[1,7168]{1,0:T(1,128)} %bitcast.6, bf16[1,576,7168]{2,1,0:T(8,128)(2,1)} %bitcast.4, bf16[1,576,7168]{2,1,0:T(8,128)(2,1)} %bitcast.5, bf16[1,576,7168]{2,1,0:T(8,128)(2,1)} %down_hbm.1), custom_call_target="tpu_custom_call" | custom-call | tf_op jit(solution)/shard_map/pallas_call | solution.py:616
  148.5 1.8 %copy.8 = bf16[32,7168]{1,0:T(8,128)(2,1)} copy(bf16[32,7168]{1,0:T(8,128)(2,1)} %shard_map.64) | data formatting | bytes 917504
